TPU v7x, 256 devices: a whole 4x4x8 slice. The times are simulated.
256 devices in a mesh: dp: 4 (over y), expert: 64 (over z, x, core).
Axes of the slice: x: 4, y: 4, z: 8, core: 2. Of those that a mesh axis runs over, the one named last changes fastest.
Arguments:
- tokens: bfloat16 [8192, 4096], P('expert', 'dp'), may hold values from -6 to 6
- grad_out: bfloat16 [8192, 4096], P('expert', 'dp'), may hold values from -6 to 6
- route_weights: bfloat16 [8192, 2], P('expert'), may hold values from 0.049804688 to 1
- expert_ids: int32 [8192, 2], P('expert'), may hold values from 0 to 63, all different within a row; in each aligned block of 128 rows (0 to 127, 128 to 255, ...) at most 8 rows name the same one
- gate_weight: bfloat16 [64, 4096, 1024], P('expert', None, 'dp'), may hold values from -0.09375 to 0.09375
- up_weight: bfloat16 [64, 4096, 1024], P('expert', None, 'dp'), may hold values from -0.09375 to 0.09375
- down_weight: bfloat16 [64, 1024, 4096], P('expert', 'dp'), may hold values from -0.1875 to 0.1875
Outputs:
- grad_tokens: bfloat16 [8192, 4096], P('expert', 'dp')
- grad_gate: bfloat16 [64, 4096, 1024], P('expert', None, 'dp')
- grad_up: bfloat16 [64, 4096, 1024], P('expert', None, 'dp')
- grad_down: bfloat16 [64, 1024, 4096], P('expert', 'dp')
Inputs may be any that keep to these rules, and one draw needn't show every extreme that they name: `expert_ids`: each row names 2 different experts. Among the 128 rows of one device no expert is named more than 8 times, and in some such block an expert is named exactly 8 times.
All inputs are finite; a program needn't handle non-finite values.
Results may differ from a plain program's by a relative error of at most 0.0057.
Values may be sent and summed in bfloat16 or wider, within the bound.
A program may use at most 128 MiB of HBM per device.

v0:
```python
import jax
import jax.numpy as jnp
from jax import lax
from jax.sharding import PartitionSpec as P


def pick_rows(source_rows, token_of, filled, experts, capacity):
    taken_rows = jnp.take(source_rows, token_of, axis=0)
    kept_rows = jnp.where(filled[:, None], taken_rows, jnp.zeros((), source_rows.dtype))
    return kept_rows.reshape(experts, capacity, source_rows.shape[1])


def combine_slots(returned, target, tok_rows, top_count):
    flat_rows = returned.reshape(-1, returned.shape[2])
    gathered = jnp.take(flat_rows, target, axis=0)
    return jnp.sum(gathered.reshape(tok_rows, top_count, flat_rows.shape[1]), axis=1)


def contract_rows(left, right):
    return lax.dot_general(
        left, right, (((0,), (0,)), ((), ())), preferred_element_type=jnp.float32
    )


def contract_last(left, right):
    return lax.dot_general(
        left, right, (((1,), (1,)), ((), ())), preferred_element_type=jnp.float32
    )


def body(tokens, grad_out, route_weights, expert_ids, gate_weight, up_weight, down_weight):
    tok_rows = tokens.shape[0]
    top_count = expert_ids.shape[1]
    experts = lax.axis_size("expert")
    capacity = 2 * tok_rows * top_count // experts
    flat_ids = expert_ids.reshape(-1)
    assignments = flat_ids.shape[0]
    onehot = (flat_ids[:, None] == jnp.arange(experts, dtype=jnp.int32)[None, :]).astype(jnp.int32)
    earlier = jnp.cumsum(onehot, axis=0) - onehot
    slot_index = jnp.sum(earlier * onehot, axis=1)
    target = flat_ids * capacity + slot_index
    matches = target[None, :] == jnp.arange(experts * capacity, dtype=jnp.int32)[:, None]
    filled = jnp.any(matches, axis=1)
    source = jnp.sum(
        jnp.where(matches, jnp.arange(assignments, dtype=jnp.int32)[None, :], 0), axis=1
    )
    token_of = source // top_count
    slot_weight = jnp.where(
        filled, route_weights.reshape(-1)[source], jnp.zeros((), route_weights.dtype)
    )
    slot_weight = slot_weight.reshape(experts, capacity)
    whole_in, whole_grad = (
        lax.all_gather(tokens, "dp", axis=1, tiled=True),
        lax.all_gather(grad_out, "dp", axis=1, tiled=True),
    )
    rows_in, rows_grad, rows_weight = (
        lax.all_to_all(
            pick_rows(whole_in, token_of, filled, experts, capacity),
            "expert",
            split_axis=0,
            concat_axis=0,
            tiled=True,
        ),
        lax.all_to_all(
            pick_rows(whole_grad, token_of, filled, experts, capacity),
            "expert",
            split_axis=0,
            concat_axis=0,
            tiled=True,
        ),
        lax.all_to_all(slot_weight, "expert", split_axis=0, concat_axis=0, tiled=True),
    )
    senders = rows_in.shape[0]
    feature_count = rows_in.shape[2]
    row_count = senders * capacity
    flat_in = rows_in.reshape(row_count, feature_count)
    flat_grad = rows_grad.reshape(row_count, feature_count)
    flat_weight = rows_weight.reshape(row_count, 1)
    gate_matrix = gate_weight[0]
    up_matrix = up_weight[0]
    down_matrix = down_weight[0]
    gate_pre = jnp.dot(flat_in, gate_matrix, preferred_element_type=jnp.float32)
    up_pre = jnp.dot(flat_in, up_matrix, preferred_element_type=jnp.float32)
    sigmoid_gate = jax.nn.sigmoid(gate_pre)
    swish_gate = gate_pre * sigmoid_gate
    activated = (swish_gate * up_pre).astype(jnp.bfloat16)
    scaled = (flat_weight.astype(jnp.float32) * flat_grad.astype(jnp.float32)).astype(jnp.bfloat16)
    grad_act = contract_last(scaled, down_matrix)
    grad_gate_pre = (
        grad_act * up_pre * sigmoid_gate * (1.0 + gate_pre * (1.0 - sigmoid_gate))
    ).astype(jnp.bfloat16)
    grad_up_pre = (grad_act * swish_gate).astype(jnp.bfloat16)
    grad_down = contract_rows(activated, scaled).astype(jnp.bfloat16)
    grad_gate = contract_rows(flat_in, grad_gate_pre).astype(jnp.bfloat16)
    grad_up = contract_rows(flat_in, grad_up_pre).astype(jnp.bfloat16)
    back_terms = contract_last(grad_gate_pre, gate_matrix) + contract_last(grad_up_pre, up_matrix)
    back_terms = back_terms.reshape(senders, capacity, feature_count)
    returned = lax.all_to_all(back_terms, "expert", split_axis=0, concat_axis=0, tiled=True)
    per_token = combine_slots(returned, target, tok_rows, top_count)
    grad_tokens = lax.psum_scatter(per_token, "dp", scatter_dimension=1, tiled=True)
    return (grad_tokens.astype(jnp.bfloat16), grad_gate[None], grad_up[None], grad_down[None])


def solution(mesh):
    placed = (
        P("expert", "dp"),
        P("expert", "dp"),
        P("expert", None),
        P("expert", None),
        P("expert", None, "dp"),
        P("expert", None, "dp"),
        P("expert", "dp", None),
    )
    return jax.shard_map(
        body,
        mesh=mesh,
        in_specs=placed,
        out_specs=(
            P("expert", "dp"),
            P("expert", None, "dp"),
            P("expert", None, "dp"),
            P("expert", "dp", None),
        ),
        check_vma=False,
    )
```

profile of v0, /device:TPU:1, one launch (start us, length us, event | category | flops | bytes accessed | tf_op | source)
XLA Modules:
  0.0 558.3 jit_solution(1370415668278301566)
XLA Ops:
  7.2 0.7 all-gather.5.cloned.1.call-update
  8.0 0.7 all-gather.3.cloned.1.call-update
  8.7 0.8 copy.29
  9.7 0.8 copy.34
  10.7 0.6 reduce-window.6
  11.8 3.4 gather_fusion
  15.4 0.7 select_n.85
  16.1 13.0 %all-to-all-start = ((bf16[64,1,8]{2,1,0:T(2,128)(2,1)}), bf16[64,1,8]{2,1,0:T(2,128)(2,1)S(1)}, u32[]{:S(2)}, u32[]{:S(2)}) async-start(bf16[64,1,8]{2,1,0:T(2,128)(2,1)} %select_n.85), calls=%async_computation | async-start | bytes 65536 | tf_op jit(solution)/shard_map/all_to_all | solution.py:71
  29.1 10.2 %all-gather.5.cloned.1.call-done = bf16[128,4096]{1,0:T(8,128)(2,1)} async-done(((bf16[128,1024]{1,0:T(8,128)(2,1)}), bf16[128,4096]{1,0:T(8,128)(2,1)}) %all-gather.5.cloned.1.call-update) | async-done | bytes 1048592 | tf_op jit(solution)/shard_map/all_gather | solution.py:53
  39.3 9.9 %gather_fusion.3 = bf16[512,4096]{1,0:T(8,128)(2,1)} fusion(bf16[128,4096]{1,0:T(8,128)(2,1)} %all-gather.5.cloned.1.call-done, s32[1024]{0:T(1024)S(1)} %pad_clamp_fusion.1), kind=kCustom, calls=%fused_computation.1.clone | custom fusion | bytes 8390656 | tf_op jit(solution)/shard_map/jit(_take)/gather | solution.py:8
  49.2 18.8 %all-gather.3.cloned.1.call-done = bf16[128,4096]{1,0:T(8,128)(2,1)} async-done(((bf16[128,1024]{1,0:T(8,128)(2,1)}), bf16[128,4096]{1,0:T(8,128)(2,1)}) %all-gather.3.cloned.1.call-update) | async-done | bytes 1048592 | tf_op jit(solution)/shard_map/all_gather | solution.py:54
  68.0 9.9 %gather_fusion.2 = bf16[512,4096]{1,0:T(8,128)(2,1)} fusion(bf16[128,4096]{1,0:T(8,128)(2,1)} %all-gather.3.cloned.1.call-done, s32[1024]{0:T(1024)S(1)} %pad_clamp_fusion.1), kind=kCustom, calls=%fused_computation.clone | custom fusion | bytes 8390656 | tf_op jit(solution)/shard_map/jit(_take)/gather | solution.py:8
  77.9 6.0 %fusion.17 = (bf16[64,8,4096]{2,1,0:T(8,128)(2,1)}, bf16[64,8,4096]{2,1,0:T(8,128)(2,1)}) fusion(bf16[512,4096]{1,0:T(8,128)(2,1)} %gather_fusion.2, pred[512]{0:T(512)(128)(4,1)S(1)} %get-tuple-element.5, pred[512]{0:T(512)(128)(4,1)S(1)} %fusion.27, bf16[512,4096]{1,0:T(8,128)(2,1)} %gather_fusion.3), kind=kLoop, calls=%fused_computation.27 | loop fusion | flops 8388608 | bytes 16778240 | tf_op jit(solution)/shard_map/reshape | solution.py:10
  83.9 106.3 %all_to_all.21 = bf16[64,8,4096]{2,1,0:T(8,128)(2,1)} all-to-all(bf16[64,8,4096]{2,1,0:T(8,128)(2,1)} %get-tuple-element.10), channel_id=1, replica_groups=mesh['dp'=4,'expert'=64] {'expert'}, dimensions={0} | all-to-all | bytes 8388608 | tf_op jit(solution)/shard_map/all_to_all | solution.py:57
  190.2 7.4 %all-to-all-start.1 = ((bf16[64,8,4096]{2,1,0:T(8,128)(2,1)}), bf16[64,8,4096]{2,1,0:T(8,128)(2,1)}, u32[]{:S(2)}, u32[]{:S(2)}) async-start(bf16[64,8,4096]{2,1,0:T(8,128)(2,1)} %get-tuple-element.9), calls=%async_computation.1 | async-start | bytes 8388608 | tf_op jit(solution)/shard_map/all_to_all | solution.py:64
  197.7 3.6 fusion.12
  201.3 0.5 copy-done.4
  201.8 2.0 fusion.14
  203.8 88.4 %all-to-all-done.1 = bf16[64,8,4096]{2,1,0:T(8,128)(2,1)} async-done(((bf16[64,8,4096]{2,1,0:T(8,128)(2,1)}), bf16[64,8,4096]{2,1,0:T(8,128)(2,1)}, u32[]{:S(2)}, u32[]{:S(2)}) %all-to-all-start.1) | async-done | bytes 4194336 | tf_op jit(solution)/shard_map/all_to_all | solution.py:64
  292.2 4.3 multiply_convert_fusion.1
  296.5 1.3 fusion.20
  298.1 4.6 add_bitcast_fusion
  302.7 7.5 %all-to-all-start.3 = ((f32[64,8,4096]{2,1,0:T(8,128)}), f32[64,8,4096]{2,1,0:T(8,128)}, u32[]{:S(2)}, u32[]{:S(2)}) async-start(f32[64,8,4096]{2,1,0:T(8,128)} %add_bitcast_fusion), calls=%async_computation.3 | async-start | bytes 16777216 | tf_op jit(solution)/shard_map/all_to_all | solution.py:98
  310.9 182.2 %all-to-all-done.3 = f32[64,8,4096]{2,1,0:T(8,128)} async-done(((f32[64,8,4096]{2,1,0:T(8,128)}), f32[64,8,4096]{2,1,0:T(8,128)}, u32[]{:S(2)}, u32[]{:S(2)}) %all-to-all-start.3) | async-done | bytes 8388640 | tf_op jit(solution)/shard_map/all_to_all | solution.py:98
  493.1 9.0 %gather_fusion.1 = f32[256,4096]{1,0:T(8,128)} fusion(f32[512,4096]{1,0:T(8,128)} %bitcast.12, s32[1024]{0:T(1024)S(1)} %pad_clamp_fusion), kind=kCustom, calls=%fused_computation.3 | custom fusion | bytes 8389632 | tf_op jit(solution)/shard_map/jit(_take)/gather | solution.py:15
  502.1 5.8 %gather.14 = f32[128,2,4096]{2,1,0:T(2,128)} reshape(f32[256,4096]{1,0:T(8,128)} %gather_fusion.1) | data formatting | bytes 8388608 | tf_op jit(solution)/shard_map/jit(_take)/gather | solution.py:15
  508.0 10.1 %select_reduce_fusion = f32[128,4096]{1,0:T(8,128)} fusion(f32[128,2,4096]{2,1,0:T(2,128)} %gather.14, pred[128,2]{1,0:T(8,128)(4,1)S(1)} %copy.33), kind=kLoop, calls=%fused_computation.29 | loop fusion | flops 1572864 | bytes 6291712 | tf_op jit(solution)/shard_map/reduce_sum | solution.py:16
  518.3 5.0 fusion.4
  523.3 2.7 fusion.3
  526.0 4.9 fusion.5
  530.9 19.1 %reduce-scatter.2.cloned.1.call-done = f32[128,1024]{1,0:T(8,128)} async-done(((f32[128,4096]{1,0:T(8,128)}), f32[128,1024]{1,0:T(8,128)}) %reduce-scatter.2.cloned.1.call-update) | async-done | bytes 524304 | tf_op jit(solution)/shard_map/reduce_scatter | solution.py:100
  550.0 1.8 convert_element_type.71
  (48 shorter events, 2.4 us)
Async XLA Ops:
  7.2 190.5 %copy-start = (bf16[1,4096,256]{2,1,0:T(8,128)(2,1)S(1)}, bf16[1,4096,256]{2,1,0:T(8,128)(2,1)}, u32[]{:S(2)}) copy-start(bf16[1,4096,256]{2,1,0:T(8,128)(2,1)} %param.13) | copy-start | bytes 6291460
  7.2 32.1 %all-gather.5.cloned.1.call-start = ((), (), s32[]{:S(2)}) async-start(), calls=%async_computation.6 | async-start | bytes 1310720 | tf_op jit(solution)/shard_map/all_gather | solution.py:53
  7.9 60.1 %all-gather.3.cloned.1.call-start = ((), (), s32[]{:S(2)}) async-start(), calls=%async_computation.5 | async-start | bytes 1310720 | tf_op jit(solution)/shard_map/all_gather | solution.py:54
  16.1 67.8 %all-to-all-start = ((bf16[64,1,8]{2,1,0:T(2,128)(2,1)}), bf16[64,1,8]{2,1,0:T(2,128)(2,1)S(1)}, u32[]{:S(2)}, u32[]{:S(2)}) async-start(bf16[64,1,8]{2,1,0:T(2,128)(2,1)} %select_n.85), calls=%async_computation | async-start | bytes 65536 | tf_op jit(solution)/shard_map/all_to_all | solution.py:71
  190.2 102.0 %all-to-all-start.1 = ((bf16[64,8,4096]{2,1,0:T(8,128)(2,1)}), bf16[64,8,4096]{2,1,0:T(8,128)(2,1)}, u32[]{:S(2)}, u32[]{:S(2)}) async-start(bf16[64,8,4096]{2,1,0:T(8,128)(2,1)} %get-tuple-element.9), calls=%async_computation.1 | async-start | bytes 8388608 | tf_op jit(solution)/shard_map/all_to_all | solution.py:64
  197.6 3.7 copy-start.2
  197.6 4.1 copy-start.4
  296.5 1.6 copy-start.5
  302.7 7.7 %copy-start.6 = (s32[128,2]{0,1:T(2,128)S(1)}, s32[128,2]{0,1:T(2,128)}, u32[]{:S(2)}) copy-start(s32[128,2]{0,1:T(2,128)} %param.12) | copy-start | bytes 3076
  302.7 190.4 %all-to-all-start.3 = ((f32[64,8,4096]{2,1,0:T(8,128)}), f32[64,8,4096]{2,1,0:T(8,128)}, u32[]{:S(2)}, u32[]{:S(2)}) async-start(f32[64,8,4096]{2,1,0:T(8,128)} %add_bitcast_fusion), calls=%async_computation.3 | async-start | bytes 16777216 | tf_op jit(solution)/shard_map/all_to_all | solution.py:98
  310.2 239.7 %reduce-scatter.2.cloned.1.call-start = ((), (), s32[]{:S(2)}) async-start(), calls=%async_computation.7 | async-start | bytes 2621440 | tf_op jit(solution)/shard_map/reduce_scatter | solution.py:100
  518.3 5.0 copy-start.3
  523.3 2.7 copy-start.7
  523.3 28.4 %copy-start.1 = (bf16[1,4096,256]{2,1,0:T(8,128)(2,1)S(1)}, bf16[1,4096,256]{2,1,0:T(8,128)(2,1)}, u32[]{:S(2)}) copy-start(bf16[1,4096,256]{2,1,0:T(8,128)(2,1)} %param.13) | copy-start | bytes 6291460
Sparse Core Ops, SparseCore 0:
  9.8 29.4 all-gather.4
  41.1 26.8 all-gather.2
  518.2 31.6 reduce-scatter.1
where the time goes:
time: 559 us; the launch traced here: 558 us
  waiting for transfers between devices  320 us (57%)
  blocking collectives  106 us (19%)
  local copies, waits for them, and re-layouts  42.4 us (8%)
  matrix products  28.4 us (5%)
  starting transfers between devices  28 us (5%)
  other arithmetic  19.2 us (3%)
  between operations  14 us (3%)
    all_to_all x1, waiting for transfers between devices, body(): lax.all_to_all(back_terms, 'expert', split_axis=0, concat_axis=0, tiled=T...  182 us
    all_to_all x1, blocking collectives, body(): lax.all_to_all(pick_rows(whole_in, token_of, filled, experts, capacity),...  106 us
    all_to_all x1, waiting for transfers between devices, body(): lax.all_to_all(pick_rows(whole_grad, token_of, filled, experts, capacity)...  88.4 us
    gather x2, local copies, waits for them, and re-layouts, pick_rows(): taken_rows = jnp.take(source_rows, token_of, axis=0)  19.8 us
    reduce_scatter x1, waiting for transfers between devices, body(): lax.psum_scatter(per_token, 'dp', scatter_dimension=1, tiled=True)  19.1 us
    all_gather x1, waiting for transfers between devices, body(): lax.all_gather(grad_out, 'dp', axis=1, tiled=True)  18.8 us
    gather x2, local copies, waits for them, and re-layouts, combine_slots(): gathered = jnp.take(flat_rows, target, axis=0)  14.9 us
    all_to_all x1, starting transfers between devices, body(): lax.all_to_all(slot_weight, 'expert', split_axis=0, concat_axis=0, tiled=...  13 us
  transfers between devices with their start and end apart: 6, of which 5 were waited for; matrix products, arithmetic and copies ran while one was open for 9% of the time, Pallas kernels for 0%

commit v1 on v0

v1 whole, which is shorter than its diff:
```python
import functools

import jax
import jax.numpy as jnp
from jax import lax
from jax.experimental import pallas as pl
from jax.experimental.pallas import tpu as pltpu
from jax.sharding import PartitionSpec as P

CAP = 8
PARTS = 4
ZS, XS, CORES = 8, 4, 2
MESH = pl.DeviceIdType.MESH


def dot_last(left, right):
    return lax.dot_general(
        left, right, (((1,), (1,)), ((), ())), preferred_element_type=jnp.float32
    )


def dot_rows(left, right):
    return lax.dot_general(
        left, right, (((0,), (0,)), ((), ())), preferred_element_type=jnp.float32
    )


def kernel(
    ids_ref, weights_ref, tokens_ref, grad_ref, gate_hbm, up_hbm, down_hbm,
    out_tokens, out_gate, out_up, out_down,
    both, send, recv, tok, sca, wgu, wdn, hid, act, part,
    pair_send, pair_recv, sum_send, sum_recv, home_send, home,
    stage_gate, stage_up, stage_down,
    weight_sems, send_sems, recv_sems, own_send, fwd_send, row_sems,
    pair_out, pair_sems, sum_out, sum_sems, home_out, home_sem, write_sems,
):
    rank = lax.axis_index("expert")
    y = lax.axis_index("dp")
    plane = XS * CORES
    experts = ZS * plane
    rows = plane * CAP
    zi, xi, ci = rank // plane, (rank // CORES) % XS, rank % CORES
    right, left = (y + 1) % PARTS, (y + PARTS - 1) % PARTS
    across = (y + 2) % PARTS
    tok_rows, width = tokens_ref.shape
    half = width // 2
    hidden = act.shape[1]

    def at(row, col):
        return pl.ds(pl.multiple_of(row * col, col), col)

    def offset(k):
        return (k * (2 * (k % 2) - 1) + ZS * ZS) % ZS

    def peer(k, i, sign):
        z = (zi + sign * offset(k) + ZS) % ZS
        x = (xi + sign * (i // CORES) + XS) % XS
        c = (ci + i) % CORES
        return z * plane + x * CORES + c

    barrier = pltpu.get_barrier_semaphore()

    def greet(j, carry):
        pl.semaphore_signal(
            barrier, inc=1, device_id=(y, (rank + j) % experts), device_id_type=MESH
        )
        return carry

    lax.fori_loop(1, experts, greet, 0)
    for side in (left, right):
        pl.semaphore_signal(barrier, inc=1, device_id=(side, rank), device_id_type=MESH)

    weight_copies = [
        pltpu.make_async_copy(gate_hbm, wgu.at[:, pl.ds(0, hidden)], weight_sems.at[0]),
        pltpu.make_async_copy(up_hbm, wgu.at[:, pl.ds(hidden, hidden)], weight_sems.at[1]),
        pltpu.make_async_copy(down_hbm, wdn, weight_sems.at[2]),
    ]
    for copy in weight_copies:
        copy.start()

    both[pl.ds(0, tok_rows), :] = tokens_ref[...]
    both[pl.ds(tok_rows, tok_rows), :] = grad_ref[...]

    ids, weights = ids_ref[...], weights_ref[...].astype(jnp.float32)
    numbers = lax.broadcasted_iota(jnp.int32, (experts, tok_rows), 0)
    hits = [numbers == ids[c : c + 1] for c in range(2)]
    before = lax.broadcasted_iota(jnp.int32, (tok_rows, tok_rows), 0) < (
        lax.broadcasted_iota(jnp.int32, (tok_rows, tok_rows), 1)
    )
    earlier = jnp.dot(
        jnp.where(hits[0] | hits[1], 1.0, 0.0).astype(jnp.bfloat16),
        jnp.where(before, 1.0, 0.0).astype(jnp.bfloat16),
        preferred_element_type=jnp.float32,
    )
    place = [
        jnp.sum(jnp.where(hits[c], earlier, 0.0), axis=0, keepdims=True)
        + ids[c : c + 1].astype(jnp.float32) * (2 * CAP)
        for c in range(2)
    ]

    def chosen(z, first, second):
        line = lax.broadcasted_iota(jnp.int32, (plane * 2 * CAP, tok_rows), 0)
        line = (line + z * (plane * 2 * CAP)).astype(jnp.float32)
        halves = [
            jnp.where(line == place[0] + shift, value[0:1], 0.0)
            + jnp.where(line == place[1] + shift, value[1:2], 0.0)
            for shift, value in ((0.0, first), (float(CAP), second))
        ]
        return jnp.concatenate(halves, axis=1).astype(jnp.bfloat16)

    ones = jnp.ones_like(weights)

    def pack(k):
        z = (zi - offset(k) + ZS) % ZS
        picked = jnp.dot(
            chosen(z, ones, weights), both[...], preferred_element_type=jnp.float32
        )
        send[at(z, plane)] = picked.astype(jnp.bfloat16).reshape(plane, 2 * CAP, width)

    def row_copy(k, i):
        target = peer(k, i, -1)
        return pltpu.make_async_remote_copy(
            src_ref=send.at[target],
            dst_ref=recv.at[k * plane + i],
            send_sem=send_sems.at[k],
            recv_sem=recv_sems.at[k],
            device_id=(y, target),
            device_id_type=MESH,
        )

    def dispatch(k, first):
        def one(i, carry):
            row_copy(k, i).start()
            return carry

        lax.fori_loop(first, plane, one, 0)

    def block_wait(k, count):
        return pltpu.make_async_remote_copy(
            src_ref=send.at[pl.ds(0, count)],
            dst_ref=recv.at[pl.ds(k * plane + plane - count, count)],
            send_sem=send_sems.at[k],
            recv_sem=recv_sems.at[k],
            device_id=(right, rank),
            device_id_type=MESH,
        )

    def side_copy(buf, q, k, sem_out, sem_in, side):
        block = buf.at[q, at(k, rows)]
        return pltpu.make_async_remote_copy(
            src_ref=block,
            dst_ref=block,
            send_sem=sem_out,
            recv_sem=sem_in,
            device_id=(side, rank),
            device_id_type=MESH,
        )

    def own_copies(k):
        return [
            side_copy(tok, y, k, own_send.at[0, k], row_sems.at[0, k], right),
            side_copy(sca, y, k, own_send.at[3, k], row_sems.at[3, k], left),
            side_copy(sca, y, k, own_send.at[1, k], row_sems.at[1, k], right),
            side_copy(tok, y, k, own_send.at[2, k], row_sems.at[2, k], left),
        ]

    def onward_copies(k):
        return [
            side_copy(tok, left, k, fwd_send.at[0, k], row_sems.at[4, k], right),
            side_copy(sca, right, k, fwd_send.at[1, k], row_sems.at[5, k], left),
        ]

    def spread(k):
        @pl.when(k == 0)
        def _():
            block_wait(0, plane - 1).wait_recv()

        @pl.when(k > 0)
        def _():
            block_wait(k, plane).wait_recv()

        got = recv[at(k, plane)].astype(jnp.float32)
        mine = at(k, rows)
        tok[y, mine, :] = got[:, :CAP, :].reshape(rows, width).astype(jnp.bfloat16)
        sca[y, mine, :] = got[:, CAP:, :].reshape(rows, width).astype(jnp.bfloat16)
        for copy in own_copies(k):
            copy.start()

    def onward(k):
        copies = onward_copies(k)
        side_copy(tok, left, k, own_send.at[0, k], row_sems.at[0, k], right).wait_recv()
        copies[0].start()
        side_copy(sca, right, k, own_send.at[3, k], row_sems.at[3, k], left).wait_recv()
        copies[1].start()

    def pair_copy(s, k, side):
        return pltpu.make_async_remote_copy(
            src_ref=pair_send.at[s, k],
            dst_ref=pair_recv.at[s, k],
            send_sem=pair_out.at[s, k],
            recv_sem=pair_sems.at[s, k],
            device_id=(side, rank),
            device_id_type=MESH,
        )

    def sum_copy(s, k, side):
        return pltpu.make_async_remote_copy(
            src_ref=sum_send.at[s, k],
            dst_ref=sum_recv.at[s, k],
            send_sem=sum_out.at[s, k],
            recv_sem=sum_sems.at[s, k],
            device_id=(side, rank),
            device_id_type=MESH,
        )

    def back_part(k, q):
        mine = at(k, rows)
        return dot_last(hid[mine, :], wgu[at(q, width), :])

    def compute(k):
        mine = at(k, rows)
        side_copy(sca, left, k, own_send.at[1, k], row_sems.at[1, k], right).wait_recv()
        side_copy(tok, right, k, own_send.at[2, k], row_sems.at[2, k], left).wait_recv()
        side_copy(tok, across, k, fwd_send.at[0, k], row_sems.at[4, k], right).wait_recv()
        side_copy(sca, across, k, fwd_send.at[1, k], row_sems.at[5, k], left).wait_recv()
        pre = jnp.zeros((rows, 2 * hidden), jnp.float32)
        grad_act = jnp.zeros((rows, hidden), jnp.float32)
        for q in range(PARTS):
            pre += jnp.dot(
                tok[q, mine, :], wgu[pl.ds(q * width, width), :],
                preferred_element_type=jnp.float32,
            )
            grad_act += dot_last(sca[q, mine, :], wdn[:, pl.ds(q * width, width)])
        gate_pre, up_pre = pre[:, :hidden], pre[:, hidden:]
        sigmoid_gate = 1.0 / (1.0 + jnp.exp(-gate_pre))
        swish_gate = gate_pre * sigmoid_gate
        act[mine, :] = (swish_gate * up_pre).astype(jnp.bfloat16)
        hid[mine, :] = jnp.concatenate(
            [
                grad_act * up_pre * sigmoid_gate * (1.0 + gate_pre * (1.0 - sigmoid_gate)),
                grad_act * swish_gate,
            ],
            axis=1,
        ).astype(jnp.bfloat16)
        far = back_part(k, across).astype(jnp.bfloat16)
        pair_send[0, k] = far[:, :half]
        pair_send[1, k] = far[:, half:]
        pair_copy(0, k, right).start()
        pair_copy(1, k, left).start()
        part[0, mine, :] = back_part(k, right)
        part[1, mine, :] = back_part(k, left)
        part[2, mine, :] = back_part(k, y)

    def reduce_sides(k):
        mine = at(k, rows)
        pair_copy(0, k, right).wait_recv()
        near = part[0, mine, :]
        sum_send[0, k] = jnp.concatenate(
            [near[:, :half] + pair_recv[0, k].astype(jnp.float32), near[:, half:]], axis=1
        ).astype(jnp.bfloat16)
        sum_copy(0, k, right).start()
        pair_copy(1, k, left).wait_recv()
        near = part[1, mine, :]
        sum_send[1, k] = jnp.concatenate(
            [near[:, :half], near[:, half:] + pair_recv[1, k].astype(jnp.float32)], axis=1
        ).astype(jnp.bfloat16)
        sum_copy(1, k, left).start()

    def home_copy(k, i):
        target = peer(k, i, 1)
        return pltpu.make_async_remote_copy(
            src_ref=home_send.at[k * plane + i],
            dst_ref=home.at[rank],
            send_sem=home_out.at[k],
            recv_sem=home_sem.at[0],
            device_id=(y, target),
            device_id_type=MESH,
        )

    def go_home(k):
        mine = at(k, rows)
        sum_copy(0, k, right).wait_recv()
        sum_copy(1, k, left).wait_recv()
        total = (
            part[2, mine, :]
            + sum_recv[0, k].astype(jnp.float32)
            + sum_recv[1, k].astype(jnp.float32)
        ).reshape(plane, CAP, width)
        home_send[at(k, plane)] = jnp.concatenate(
            [total[:, :, :half], total[:, :, half:]], axis=1
        ).astype(jnp.bfloat16)

        def one(i, carry):
            home_copy(k, i).start()
            return carry

        @pl.when(k == 0)
        def _():
            home[rank] = home_send[0]
            lax.fori_loop(1, plane, one, 0)

        @pl.when(k > 0)
        def _():
            lax.fori_loop(0, plane, one, 0)

    def write_copies(q):
        lines = pl.ds(pl.multiple_of(q * width, width), width)
        return [
            pltpu.make_async_copy(stage_gate.at[lines], out_gate.at[lines], write_sems.at[0, q]),
            pltpu.make_async_copy(stage_up.at[lines], out_up.at[lines], write_sems.at[1, q]),
            pltpu.make_async_copy(
                stage_down.at[:, lines], out_down.at[:, lines], write_sems.at[2, q]
            ),
        ]

    def weight_grads(q):
        tile = min(256, width)

        def one(j, carry):
            cols = at(j, tile)
            lines = pl.ds(pl.multiple_of(q * width + j * tile, tile), tile)
            grads = dot_rows(tok[q, :, cols], hid[...]).astype(jnp.bfloat16)
            stage_gate[lines, :] = grads[:, :hidden]
            stage_up[lines, :] = grads[:, hidden:]
            stage_down[:, lines] = dot_rows(act[...], sca[q, :, cols]).astype(jnp.bfloat16)
            return carry

        lax.fori_loop(0, width // tile, one, 0)
        for copy in write_copies(q):
            copy.start()

    pack(0)
    recv[0] = send[rank]
    pl.semaphore_wait(barrier, experts + 1)
    dispatch(0, 1)

    for copy in weight_copies:
        copy.wait()

    def turn(t, carry):
        @pl.when(t < ZS)
        def _():
            spread(t)

        def ahead(first, last):
            def one(k, carry):
                pack(k)
                dispatch(k, 0)
                return carry

            lax.fori_loop(first, last, one, 0)

        @pl.when(t == 0)
        def _():
            ahead(1, min(4, ZS))

        @pl.when(t == 1)
        def _():
            ahead(min(4, ZS), min(6, ZS))

        @pl.when((t >= 2) & (t + 4 < ZS))
        def _():
            ahead(t + 4, t + 5)

        @pl.when((t >= 1) & (t < ZS + 1))
        def _():
            onward(t - 1)

        @pl.when((t >= 3) & (t < ZS + 3))
        def _():
            reduce_sides(t - 3)

        @pl.when((t >= 4) & (t < ZS + 4))
        def _():
            go_home(t - 4)

        @pl.when((t >= 2) & (t < ZS + 2))
        def _():
            compute(t - 2)

        @pl.when(t == ZS + 1)
        def _():
            weight_grads(0)

        @pl.when(t == ZS + 2)
        def _():
            weight_grads(1)

        return carry

    lax.fori_loop(0, ZS + 4, turn, 0)
    weight_grads(2)
    weight_grads(3)

    pltpu.make_async_remote_copy(
        src_ref=home_send.at[pl.ds(0, experts - 1)],
        dst_ref=home.at[pl.ds(0, experts - 1)],
        send_sem=home_out.at[0],
        recv_sem=home_sem.at[0],
        device_id=(right, rank),
        device_id_type=MESH,
    ).wait_recv()
    result = jnp.zeros((2 * tok_rows, half), jnp.float32)
    for z in range(ZS):
        block = home[pl.ds(z * plane, plane)].reshape(plane * 2 * CAP, half)
        result += dot_rows(chosen(z, ones, ones), block)
    result = result.astype(jnp.bfloat16)
    out_tokens[:, pl.ds(0, half)] = result[:tok_rows]
    out_tokens[:, pl.ds(half, half)] = result[tok_rows:]

    def finish(k, carry):
        for copy in own_copies(k) + onward_copies(k):
            copy.wait_send()
        for s, side in ((0, right), (1, left)):
            pair_copy(s, k, side).wait_send()
            sum_copy(s, k, side).wait_send()
        return carry

    lax.fori_loop(0, ZS, finish, 0)

    def sent(k, count):
        block_wait(k, count).wait_send()
        pltpu.make_async_remote_copy(
            src_ref=home_send.at[pl.ds(0, count)],
            dst_ref=home.at[pl.ds(0, count)],
            send_sem=home_out.at[k],
            recv_sem=home_sem.at[0],
            device_id=(right, rank),
            device_id_type=MESH,
        ).wait_send()

    sent(0, plane - 1)

    def finish_blocks(k, carry):
        sent(k, plane)
        return carry

    lax.fori_loop(1, ZS, finish_blocks, 0)
    for q in range(PARTS):
        for copy in write_copies(q):
            copy.wait()


def body(tokens, grad_out, route_weights, expert_ids, gate_weight, up_weight, down_weight):
    tok_rows, width = tokens.shape
    experts = lax.axis_size("expert")
    plane = XS * CORES
    rows = plane * CAP
    total = experts * CAP
    features, hidden = gate_weight.shape[1:]
    half = width // 2
    bf16, f32 = jnp.bfloat16, jnp.float32
    vmem, free = pl.BlockSpec(memory_space=pltpu.VMEM), pl.BlockSpec(memory_space=pl.ANY)
    hbm = pl.BlockSpec(memory_space=pltpu.HBM)
    dma = pltpu.SemaphoreType.DMA
    grads = pl.pallas_call(
        kernel,
        out_shape=(
            jax.ShapeDtypeStruct((tok_rows, width), bf16),
            jax.ShapeDtypeStruct((features, hidden), bf16),
            jax.ShapeDtypeStruct((features, hidden), bf16),
            jax.ShapeDtypeStruct((hidden, features), bf16),
        ),
        in_specs=[vmem, vmem, vmem, vmem, hbm, hbm, hbm],
        out_specs=(vmem, free, free, free),
        scratch_shapes=[
            pltpu.VMEM((2 * tok_rows, width), bf16),
            pltpu.VMEM((experts, 2 * CAP, width), bf16),
            pltpu.VMEM((experts, 2 * CAP, width), bf16),
            pltpu.VMEM((PARTS, total, width), bf16),
            pltpu.VMEM((PARTS, total, width), bf16),
            pltpu.VMEM((features, 2 * hidden), bf16),
            pltpu.VMEM((hidden, features), bf16),
            pltpu.VMEM((total, 2 * hidden), bf16),
            pltpu.VMEM((total, hidden), bf16),
            pltpu.VMEM((3, total, width), f32),
            pltpu.VMEM((2, ZS, rows, half), bf16),
            pltpu.VMEM((2, ZS, rows, half), bf16),
            pltpu.VMEM((2, ZS, rows, width), bf16),
            pltpu.VMEM((2, ZS, rows, width), bf16),
            pltpu.VMEM((experts, 2 * CAP, half), bf16),
            pltpu.VMEM((experts, 2 * CAP, half), bf16),
            pltpu.VMEM((features, hidden), bf16),
            pltpu.VMEM((features, hidden), bf16),
            pltpu.VMEM((hidden, features), bf16),
            dma((3,)),
            dma((ZS,)),
            dma((ZS,)),
            dma((4, ZS)),
            dma((2, ZS)),
            dma((6, ZS)),
            dma((2, ZS)),
            dma((2, ZS)),
            dma((2, ZS)),
            dma((2, ZS)),
            dma((ZS,)),
            dma((1,)),
            dma((3, PARTS)),
        ],
        compiler_params=pltpu.CompilerParams(
            collective_id=0, has_side_effects=True, vmem_limit_bytes=44 * 1024 * 1024
        ),
    )(
        expert_ids.T, route_weights.T, tokens, grad_out,
        gate_weight[0], up_weight[0], down_weight[0],
    )
    return (grads[0], grads[1][None], grads[2][None], grads[3][None])


def solution(mesh):
    placed = (
        P("expert", "dp"),
        P("expert", "dp"),
        P("expert", None),
        P("expert", None),
        P("expert", None, "dp"),
        P("expert", None, "dp"),
        P("expert", "dp", None),
    )
    return jax.shard_map(
        body,
        mesh=mesh,
        in_specs=placed,
        out_specs=(
            P("expert", "dp"),
            P("expert", None, "dp"),
            P("expert", None, "dp"),
            P("expert", "dp", None),
        ),
        check_vma=False,
    )
```

time: 559 us -> 151 us (0.27)
  waiting for transfers between devices: 320 us -> 0 us
  Pallas kernels: 0 us -> 140 us
  blocking collectives: 106 us -> 0 us
  local copies, waits for them, and re-layouts: 42.4 us -> 9.48 us
  matrix products: 28.4 us -> 0 us
  starting transfers between devices: 28 us -> 0 us
  other arithmetic: 19.2 us -> 0 us
  between operations: 14 us -> 0.66 us
    all_to_all x3 -> x0, waiting for transfers between devices: 271 us -> none  [the longest x1 182 us: body(): lax.all_to_all(back_terms, 'expert', split_axis=0, concat_axis=0, tiled=T...]
    pallas_call x0 -> x1, Pallas kernels: none -> 140 us  [body(): pl.pallas_call(kernel, out_shape=(jax.ShapeDtypeStruct((tok_rows, width),...]
    all_to_all x1 -> x0, blocking collectives: 106 us -> none  [body(): lax.all_to_all(pick_rows(whole_in, token_of, filled, experts, capacity),...]
    gather x5 -> x0, local copies, waits for them, and re-layouts: 38.1 us -> none  [the longest x2 19.8 us: pick_rows(): taken_rows = jnp.take(source_rows, token_of, axis=0)]
    all_gather x2 -> x0, waiting for transfers between devices: 29 us -> none  [the longest x1 18.8 us: body(): lax.all_gather(grad_out, 'dp', axis=1, tiled=True)]
    dot_general x8 -> x0, matrix products: 28.4 us -> none  [the longest x3 12.6 us: contract_rows(): lax.dot_general(left, right, (((0,), (0,)), ((), ())), preferred_element_...]
    all_to_all x3 -> x0, starting transfers between devices: 27.8 us -> none  [the longest x1 13 us: body(): lax.all_to_all(slot_weight, 'expert', split_axis=0, concat_axis=0, tiled=...]
    reduce_scatter x1 -> x0, waiting for transfers between devices: 19.1 us -> none  [body(): lax.psum_scatter(per_token, 'dp', scatter_dimension=1, tiled=True)]
  transfers between devices with their start and end apart: 6 -> 0, of which waited for: 5 -> 0; matrix products, arithmetic and copies ran while one was open for 9% -> 0% of each run, Pallas kernels for 0% -> 0%
where the time goes in v1:
time: 151 us
  Pallas kernels  140 us (93%)
  local copies, waits for them, and re-layouts  9.48 us (6%)
    pallas_call x1, Pallas kernels, body(): pl.pallas_call(kernel, out_shape=(jax.ShapeDtypeStruct((tok_rows, width),...  140 us
    unnamed x14, local copies, waits for them, and re-layouts  9.48 us

profile of v1, /device:TPU:1, one launch (start us, length us, event | category | flops | bytes accessed | tf_op | source)
XLA Modules:
  0.0 150.5 jit_solution(7820681600980261465)
XLA Ops:
  0.6 0.0 copy-start
  0.6 1.6 %copy-done = bf16[1,4096,256]{2,1,0:T(8,128)(2,1)S(1)} copy-done((bf16[1,4096,256]{2,1,0:T(8,128)(2,1)S(1)}, bf16[1,4096,256]{2,1,0:T(8,128)(2,1)}, u32[]{:S(2)}) %copy-start) | copy-done | bytes 2097176
  2.2 0.0 copy-start.1
  2.2 0.9 copy-done.1
  3.2 0.0 copy-start.2
  3.2 0.9 copy-done.2
  4.1 0.0 copy-start.3
  4.1 0.7 copy-done.3
  4.8 0.0 copy-start.4
  4.8 0.7 copy-done.4
  5.5 140.4 %shard_map.102 = (bf16[128,1024]{1,0:T(8,128)(2,1)S(1)}, bf16[4096,256]{1,0:T(8,128)(2,1)S(1)}, bf16[4096,256]{1,0:T(8,128)(2,1)S(1)}, bf16[256,4096]{1,0:T(8,128)(2,1)S(1)}) custom-call(s32[2,128]{1,0:T(2,128)S(1)} %bitcast.12, bf16[2,128]{1,0:T(2,128)(2,1)S(1)} %bitcast.13, bf16[128,1024]{1,0:T(8,128)(2,1)S(1)} %copy-done.1, ...), custom_call_target="tpu_custom_call" | custom-call | tf_op jit(solution)/shard_map/pallas_call | solution.py:456
  145.9 0.7 copy.15
  146.6 1.3 copy.16
  147.9 1.3 copy.17
  149.2 1.3 copy.18
Async XLA Ops:
  0.6 1.6 %copy-start = (bf16[1,4096,256]{2,1,0:T(8,128)(2,1)S(1)}, bf16[1,4096,256]{2,1,0:T(8,128)(2,1)}, u32[]{:S(2)}) copy-start(bf16[1,4096,256]{2,1,0:T(8,128)(2,1)} %param.11) | copy-start | bytes 6291460
  2.2 0.9 copy-start.1
  3.2 0.9 copy-start.2
  4.1 0.7 copy-start.3
  4.8 0.7 copy-start.4

commit v2 on v1

v2 whole, which is shorter than its diff:
```python
import jax
import jax.numpy as jnp
from jax import lax
from jax.experimental import pallas as pl
from jax.experimental.pallas import tpu as pltpu
from jax.sharding import PartitionSpec as P

CAP = 8
PARTS = 4
ZS, XS, CORES = 8, 4, 2
MESH = pl.DeviceIdType.MESH

PLANE_OF = (2, 6, 5, 3, 7, 0, 4, 1)
PLANE_CODE = sum(place << (3 * p) for p, place in enumerate(PLANE_OF))
FAR, NEAR, SAME = 5, 3, 5
SLOTS = 4

SPREAD = (0, 1, 6)
ONWARD = (3, 4, 9)
UNPACK = (8, 9, 12)
COMPUTE = (1, 2, 5, 6, 8, 9, 11, 12)
REDUCE = (4, 5, 8, 10, 11, 12, 13, 15)
GO_HOME = (7, 8, 10, 12, 13, 14, 15, 16)
TURNS = 17


def dot_last(left, right):
    return lax.dot_general(
        left, right, (((1,), (1,)), ((), ())), preferred_element_type=jnp.float32
    )


def dot_rows(left, right):
    return lax.dot_general(
        left, right, (((0,), (0,)), ((), ())), preferred_element_type=jnp.float32
    )


def kernel(
    ids_ref, weights_ref, tokens_ref, grad_ref, gate_hbm, up_hbm, down_hbm,
    out_tokens, out_gate, out_up, out_down,
    dense, far_send, far_recv, near_send, near_recv, tok, sca, wgu, wdn, hid, act, part,
    pair_send, pair_recv, sum_send, sum_recv, home_send, home,
    weight_sems, dense_out, dense_sems, far_out, far_sems, near_out, near_sems,
    own_out, onward_out, row_sems, pair_out, pair_sems, sum_out, sum_sems,
    home_out, home_sem, write_sems,
):
    rank = lax.axis_index("expert")
    y = lax.axis_index("dp")
    plane = XS * CORES
    experts = ZS * plane
    rows = plane * CAP
    zi, xi, ci = rank // plane, (rank // CORES) % XS, rank % CORES
    right, left = (y + 1) % PARTS, (y + PARTS - 1) % PARTS
    across = (y + 2) % PARTS
    tok_rows, width = tokens_ref.shape
    half = width // 2
    hidden = act.shape[1]

    def at(row, col):
        return pl.ds(pl.multiple_of(row * col, col), col)

    def offset(p):
        return (PLANE_CODE >> (3 * p)) % 8

    def far_block(j):
        return j + 2 * (j // 4)

    def near_block(n):
        return 4 + n + n // 2

    def peer(p, i, sign):
        z = (zi + sign * offset(p) + ZS) % ZS
        x = (xi + sign * (i // CORES) + XS) % XS
        c = (ci + i) % CORES
        return z * plane + x * CORES + c

    def remote(src, dst, out, arrive, device):
        return pltpu.make_async_remote_copy(
            src_ref=src, dst_ref=dst, send_sem=out, recv_sem=arrive,
            device_id=device, device_id_type=MESH,
        )

    barrier = pltpu.get_barrier_semaphore()

    def greet(j, carry):
        pl.semaphore_signal(
            barrier, inc=1, device_id=(y, (rank + j) % experts), device_id_type=MESH
        )
        return carry

    lax.fori_loop(1, experts, greet, 0)
    for side in (left, right):
        pl.semaphore_signal(barrier, inc=1, device_id=(side, rank), device_id_type=MESH)

    weight_copies = [
        pltpu.make_async_copy(gate_hbm, wgu.at[:, pl.ds(0, hidden)], weight_sems.at[0]),
        pltpu.make_async_copy(up_hbm, wgu.at[:, pl.ds(hidden, hidden)], weight_sems.at[1]),
        pltpu.make_async_copy(down_hbm, wdn, weight_sems.at[2]),
    ]
    for copy in weight_copies:
        copy.start()

    dense[y, pl.ds(0, tok_rows), :] = tokens_ref[...]
    dense[y, pl.ds(tok_rows, tok_rows), :] = grad_ref[...]

    def dense_copy(h, q, out, arrive, side):
        block = dense.at[q, pl.ds(h * tok_rows, tok_rows)]
        return remote(block, block, out, dense_sems.at[arrive], (side, rank))

    def dense_own():
        return [
            dense_copy(0, y, dense_out.at[0], 0, right),
            dense_copy(1, y, dense_out.at[1], 3, left),
            dense_copy(1, y, dense_out.at[2], 1, right),
            dense_copy(0, y, dense_out.at[3], 2, left),
        ]

    def dense_onward():
        return [
            dense_copy(0, left, dense_out.at[4], 4, right),
            dense_copy(1, right, dense_out.at[5], 5, left),
        ]

    def dense_arrival(h, q, arrive):
        dense_copy(h, q, dense_out.at[0], arrive, right).wait_recv()

    ids, weights = ids_ref[...], weights_ref[...].astype(jnp.float32)
    numbers = lax.broadcasted_iota(jnp.int32, (experts, tok_rows), 0)
    hits = [numbers == ids[c : c + 1] for c in range(2)]
    before = lax.broadcasted_iota(jnp.int32, (tok_rows, tok_rows), 0) < (
        lax.broadcasted_iota(jnp.int32, (tok_rows, tok_rows), 1)
    )
    earlier = jnp.dot(
        jnp.where(hits[0] | hits[1], 1.0, 0.0).astype(jnp.bfloat16),
        jnp.where(before, 1.0, 0.0).astype(jnp.bfloat16),
        preferred_element_type=jnp.float32,
    )
    place = [
        jnp.sum(jnp.where(hits[c], earlier, 0.0), axis=0, keepdims=True)
        + ids[c : c + 1].astype(jnp.float32) * (2 * CAP)
        for c in range(2)
    ]

    def chosen(z, first, second):
        line = lax.broadcasted_iota(jnp.int32, (plane * 2 * CAP, tok_rows), 0)
        line = (line + z * (plane * 2 * CAP)).astype(jnp.float32)
        halves = [
            jnp.where(line == place[0] + shift, value[0:1], 0.0)
            + jnp.where(line == place[1] + shift, value[1:2], 0.0)
            for shift, value in ((0.0, first), (float(CAP), second))
        ]
        return jnp.concatenate(halves, axis=1).astype(jnp.bfloat16)

    ones = jnp.ones_like(weights)

    def picks(p):
        return chosen((zi - offset(p) + ZS) % ZS, ones, weights)

    def pick(which, q):
        picked = jnp.dot(which, dense[q], preferred_element_type=jnp.float32)
        return picked.astype(jnp.bfloat16).reshape(plane, 2 * CAP, width)

    def far_copy(j, i):
        target = peer(far_block(j), i, -1)
        return remote(
            far_send.at[j, target % plane], far_recv.at[j, i],
            far_out.at[j], far_sems.at[j], (y, target),
        )

    def far_whole(j):
        return remote(far_send.at[j], far_recv.at[j], far_out.at[j], far_sems.at[j], (right, rank))

    def pack_far(j):
        far_send[j] = pick(picks(far_block(j)), y)

    def dispatch_far(j, carry):
        def one(i, inner):
            far_copy(j, i).start()
            return inner

        return lax.fori_loop(0, plane, one, carry)

    def near_copy(n, i):
        target = peer(near_block(n), i, -1)
        return remote(
            near_send.at[n, target % plane], near_recv.at[n, i],
            near_out.at[n], near_sems.at[n], (y, target),
        )

    def near_whole(n, first):
        some = pl.ds(first, plane - first)
        return remote(
            near_send.at[n, some], near_recv.at[n, some],
            near_out.at[n], near_sems.at[n], (right, rank),
        )

    def dispatch_near(n, carry):
        which = picks(near_block(n))
        for q in range(PARTS):
            near_send[n, :, q] = pick(which, q)

        def one(i, inner):
            near_copy(n, i).start()
            return inner

        same = near_block(n) == SAME

        @pl.when(same)
        def _():
            near_recv[n, 0] = near_send[n, rank % plane]
            lax.fori_loop(1, plane, one, 0)

        @pl.when(jnp.logical_not(same))
        def _():
            lax.fori_loop(0, plane, one, 0)

        return carry

    def side_copy(buf, q, p, out, arrive, side):
        block = buf.at[q, at(p, rows)]
        return remote(block, block, out, arrive, (side, rank))

    def own_copies(j):
        p = far_block(j)
        return [
            side_copy(tok, y, p, own_out.at[0, j], row_sems.at[0, j], right),
            side_copy(sca, y, p, own_out.at[1, j], row_sems.at[3, j], left),
            side_copy(sca, y, p, own_out.at[2, j], row_sems.at[1, j], right),
            side_copy(tok, y, p, own_out.at[3, j], row_sems.at[2, j], left),
        ]

    def onward_copies(j):
        p = far_block(j)
        return [
            side_copy(tok, left, p, onward_out.at[0, j], row_sems.at[4, j], right),
            side_copy(sca, right, p, onward_out.at[1, j], row_sems.at[5, j], left),
        ]

    def arrival(buf, q, j, arrive):
        side_copy(
            buf, q, far_block(j), own_out.at[0, j], row_sems.at[arrive, j], right
        ).wait_recv()

    def separate(got, q, p):
        got = got.astype(jnp.float32)
        mine = at(p, rows)
        tok[q, mine, :] = got[:, :CAP, :].reshape(rows, width).astype(jnp.bfloat16)
        sca[q, mine, :] = got[:, CAP:, :].reshape(rows, width).astype(jnp.bfloat16)

    def spread(j):
        far_whole(j).wait_recv()
        separate(far_recv[j], y, far_block(j))
        for copy in own_copies(j):
            copy.start()

    def onward(j):
        copies = onward_copies(j)
        arrival(tok, left, j, 0)
        copies[0].start()
        arrival(sca, right, j, 3)
        copies[1].start()

    def unpack(n):
        p = near_block(n)

        @pl.when(p == SAME)
        def _():
            near_whole(n, 1).wait_recv()

        @pl.when(p != SAME)
        def _():
            near_whole(n, 0).wait_recv()

        for q in range(PARTS):
            separate(near_recv[n, :, q], q, p)

    def pair_copy(s, p, side):
        return remote(
            pair_send.at[s, p], pair_recv.at[s, p], pair_out.at[s, p], pair_sems.at[s, p],
            (side, rank),
        )

    def sum_copy(s, p, side):
        return remote(
            sum_send.at[s, p], sum_recv.at[s, p], sum_out.at[s, p], sum_sems.at[s, p],
            (side, rank),
        )

    def compute(p):
        mine = at(p, rows)

        @pl.when((p < 4) | (p == 6))
        def _():
            j = p - 2 * (p // 6)
            arrival(sca, left, j, 1)
            arrival(tok, right, j, 2)
            arrival(tok, across, j, 4)
            arrival(sca, across, j, 5)

        pre = jnp.zeros((rows, 2 * hidden), jnp.float32)
        grad_act = jnp.zeros((rows, hidden), jnp.float32)
        for q in range(PARTS):
            pre += jnp.dot(
                tok[q, mine, :], wgu[pl.ds(q * width, width), :],
                preferred_element_type=jnp.float32,
            )
            grad_act += dot_last(sca[q, mine, :], wdn[:, pl.ds(q * width, width)])
        gate_pre, up_pre = pre[:, :hidden], pre[:, hidden:]
        sigmoid_gate = 1.0 / (1.0 + jnp.exp(-gate_pre))
        swish_gate = gate_pre * sigmoid_gate
        act[mine, :] = (swish_gate * up_pre).astype(jnp.bfloat16)
        hid[mine, :] = jnp.concatenate(
            [
                grad_act * up_pre * sigmoid_gate * (1.0 + gate_pre * (1.0 - sigmoid_gate)),
                grad_act * swish_gate,
            ],
            axis=1,
        ).astype(jnp.bfloat16)

        def back(q):
            return dot_last(hid[mine, :], wgu[at(q, width), :])

        far = back(across).astype(jnp.bfloat16)
        pair_send[0, p] = far[:, :half]
        pair_send[1, p] = far[:, half:]
        pair_copy(0, p, right).start()
        pair_copy(1, p, left).start()
        slot = p % SLOTS
        part[slot, 0] = back(right)
        part[slot, 1] = back(left)
        part[slot, 2] = back(y)

    def reduce_sides(p):
        slot = p % SLOTS
        pair_copy(0, p, right).wait_recv()
        near = part[slot, 0]
        sum_send[0, p] = jnp.concatenate(
            [near[:, :half] + pair_recv[0, p].astype(jnp.float32), near[:, half:]], axis=1
        ).astype(jnp.bfloat16)
        sum_copy(0, p, right).start()
        pair_copy(1, p, left).wait_recv()
        near = part[slot, 1]
        sum_send[1, p] = jnp.concatenate(
            [near[:, :half], near[:, half:] + pair_recv[1, p].astype(jnp.float32)], axis=1
        ).astype(jnp.bfloat16)
        sum_copy(1, p, left).start()

    def home_copy(p, i):
        return remote(
            home_send.at[p * plane + i], home.at[rank], home_out.at[p], home_sem.at[0],
            (y, peer(p, i, 1)),
        )

    def go_home(p):
        sum_copy(0, p, right).wait_recv()
        sum_copy(1, p, left).wait_recv()
        total = (
            part[p % SLOTS, 2]
            + sum_recv[0, p].astype(jnp.float32)
            + sum_recv[1, p].astype(jnp.float32)
        ).reshape(plane, CAP, width)
        home_send[at(p, plane)] = jnp.concatenate(
            [total[:, :, :half], total[:, :, half:]], axis=1
        ).astype(jnp.bfloat16)

        def one(i, carry):
            home_copy(p, i).start()
            return carry

        @pl.when(p == SAME)
        def _():
            home[rank] = home_send[SAME * plane]
            lax.fori_loop(1, plane, one, 0)

        @pl.when(p != SAME)
        def _():
            lax.fori_loop(0, plane, one, 0)

    def write_copies(q):
        lines = pl.ds(q * width, width)
        return [
            pltpu.make_async_copy(
                wgu.at[lines, pl.ds(0, hidden)], out_gate.at[lines], write_sems.at[0, q]
            ),
            pltpu.make_async_copy(
                wgu.at[lines, pl.ds(hidden, hidden)], out_up.at[lines], write_sems.at[1, q]
            ),
            pltpu.make_async_copy(wdn.at[:, lines], out_down.at[:, lines], write_sems.at[2, q]),
        ]

    def weight_grads(q):
        tile = min(256, width)

        def one(j, carry):
            cols = at(j, tile)
            lines = pl.ds(pl.multiple_of(q * width + j * tile, tile), tile)
            wgu[lines, :] = dot_rows(tok[q, :, cols], hid[...]).astype(jnp.bfloat16)
            wdn[:, lines] = dot_rows(act[...], sca[q, :, cols]).astype(jnp.bfloat16)
            return carry

        lax.fori_loop(0, width // tile, one, 0)
        for copy in write_copies(q):
            copy.start()

    pack_far(0)
    pl.semaphore_wait(barrier, experts + 1)
    for copy in dense_own():
        copy.start()
    dispatch_far(0, 0)

    def next_far(j, carry):
        pack_far(j)
        return dispatch_far(j, carry)

    lax.fori_loop(1, 3, next_far, 0)
    copies = dense_onward()
    dense_arrival(0, left, 0)
    copies[0].start()
    dense_arrival(1, right, 3)
    copies[1].start()
    lax.fori_loop(3, FAR, next_far, 0)
    for copy in weight_copies:
        copy.wait()

    def next_spread(j, carry):
        spread(j)
        return carry

    def next_onward(j, carry):
        onward(j)
        return carry

    lax.fori_loop(0, 2, next_spread, 0)
    dense_arrival(1, left, 1)
    dense_arrival(0, right, 2)
    dense_arrival(0, across, 4)
    dense_arrival(1, across, 5)
    lax.fori_loop(0, NEAR, dispatch_near, 0)
    lax.fori_loop(0, 2, next_onward, 0)

    def turn(t, carry):
        def stage(turns, work, done):
            now = t == turns[0]
            for at_turn in turns[1:]:
                now = now | (t == at_turn)

            @pl.when(now)
            def _():
                index = done
                for at_turn in turns:
                    index = index + jnp.where(t > at_turn, 1, 0)
                work(index)

        stage(ONWARD, onward, 2)
        stage(REDUCE, reduce_sides, 0)
        stage(GO_HOME, go_home, 0)
        stage(SPREAD, spread, 2)
        stage(UNPACK, unpack, 0)
        stage(COMPUTE, compute, 0)
        return carry

    lax.fori_loop(0, TURNS, turn, 0)
    for q in range(PARTS):
        weight_grads(q)

    remote(
        home_send.at[pl.ds(0, experts - 1)], home.at[pl.ds(0, experts - 1)],
        home_out.at[0], home_sem.at[0], (right, rank),
    ).wait_recv()
    result = jnp.zeros((2 * tok_rows, half), jnp.float32)
    for z in range(ZS):
        block = home[pl.ds(z * plane, plane)].reshape(plane * 2 * CAP, half)
        result += dot_rows(chosen(z, ones, ones), block)
    result = result.astype(jnp.bfloat16)
    out_tokens[:, pl.ds(0, half)] = result[:tok_rows]
    out_tokens[:, pl.ds(half, half)] = result[tok_rows:]

    for copy in dense_own() + dense_onward():
        copy.wait_send()

    def finish_far(j, carry):
        far_whole(j).wait_send()
        for copy in own_copies(j) + onward_copies(j):
            copy.wait_send()
        return carry

    lax.fori_loop(0, FAR, finish_far, 0)
    for n in range(NEAR):
        near_whole(n, 1 if near_block(n) == SAME else 0).wait_send()

    def home_sent(p, count):
        some = pl.ds(0, count)
        remote(
            home_send.at[some], home.at[some], home_out.at[p], home_sem.at[0], (right, rank)
        ).wait_send()

    def finish(p, carry):
        for s, side in ((0, right), (1, left)):
            pair_copy(s, p, side).wait_send()
            sum_copy(s, p, side).wait_send()

        @pl.when(p == SAME)
        def _():
            home_sent(p, plane - 1)

        @pl.when(p != SAME)
        def _():
            home_sent(p, plane)

        return carry

    lax.fori_loop(0, ZS, finish, 0)
    for q in range(PARTS):
        for copy in write_copies(q):
            copy.wait()


def body(tokens, grad_out, route_weights, expert_ids, gate_weight, up_weight, down_weight):
    tok_rows, width = tokens.shape
    experts = lax.axis_size("expert")
    plane = XS * CORES
    rows = plane * CAP
    total = experts * CAP
    features, hidden = gate_weight.shape[1:]
    half = width // 2
    bf16, f32 = jnp.bfloat16, jnp.float32
    vmem, free = pl.BlockSpec(memory_space=pltpu.VMEM), pl.BlockSpec(memory_space=pl.ANY)
    hbm = pl.BlockSpec(memory_space=pltpu.HBM)
    dma = pltpu.SemaphoreType.DMA
    grads = pl.pallas_call(
        kernel,
        out_shape=(
            jax.ShapeDtypeStruct((tok_rows, width), bf16),
            jax.ShapeDtypeStruct((features, hidden), bf16),
            jax.ShapeDtypeStruct((features, hidden), bf16),
            jax.ShapeDtypeStruct((hidden, features), bf16),
        ),
        in_specs=[vmem, vmem, vmem, vmem, hbm, hbm, hbm],
        out_specs=(vmem, free, free, free),
        scratch_shapes=[
            pltpu.VMEM((PARTS, 2 * tok_rows, width), bf16),
            pltpu.VMEM((FAR, plane, 2 * CAP, width), bf16),
            pltpu.VMEM((FAR, plane, 2 * CAP, width), bf16),
            pltpu.VMEM((NEAR, plane, PARTS, 2 * CAP, width), bf16),
            pltpu.VMEM((NEAR, plane, PARTS, 2 * CAP, width), bf16),
            pltpu.VMEM((PARTS, total, width), bf16),
            pltpu.VMEM((PARTS, total, width), bf16),
            pltpu.VMEM((features, 2 * hidden), bf16),
            pltpu.VMEM((hidden, features), bf16),
            pltpu.VMEM((total, 2 * hidden), bf16),
            pltpu.VMEM((total, hidden), bf16),
            pltpu.VMEM((SLOTS, 3, rows, width), f32),
            pltpu.VMEM((2, ZS, rows, half), bf16),
            pltpu.VMEM((2, ZS, rows, half), bf16),
            pltpu.VMEM((2, ZS, rows, width), bf16),
            pltpu.VMEM((2, ZS, rows, width), bf16),
            pltpu.VMEM((experts, 2 * CAP, half), bf16),
            pltpu.VMEM((experts, 2 * CAP, half), bf16),
            dma((3,)),
            dma((6,)),
            dma((6,)),
            dma((FAR,)),
            dma((FAR,)),
            dma((NEAR,)),
            dma((NEAR,)),
            dma((4, FAR)),
            dma((2, FAR)),
            dma((6, FAR)),
            dma((2, ZS)),
            dma((2, ZS)),
            dma((2, ZS)),
            dma((2, ZS)),
            dma((ZS,)),
            dma((1,)),
            dma((3, PARTS)),
        ],
        compiler_params=pltpu.CompilerParams(
            collective_id=0, has_side_effects=True, vmem_limit_bytes=47 * 1024 * 1024
        ),
    )(
        expert_ids.T, route_weights.T, tokens, grad_out,
        gate_weight[0], up_weight[0], down_weight[0],
    )
    return (grads[0], grads[1][None], grads[2][None], grads[3][None])


def solution(mesh):
    placed = (
        P("expert", "dp"),
        P("expert", "dp"),
        P("expert", None),
        P("expert", None),
        P("expert", None, "dp"),
        P("expert", None, "dp"),
        P("expert", "dp", None),
    )
    return jax.shard_map(
        body,
        mesh=mesh,
        in_specs=placed,
        out_specs=(
            P("expert", "dp"),
            P("expert", None, "dp"),
            P("expert", None, "dp"),
            P("expert", "dp", None),
        ),
        check_vma=False,
    )
```

time: 151 us -> 138 us (0.914)
  Pallas kernels: 140 us -> 129 us
  local copies, waits for them, and re-layouts: 9.48 us -> 7.89 us
    pallas_call x1, Pallas kernels: 140 us -> 129 us  [body(): pl.pallas_call(kernel, out_shape=(jax.ShapeDtypeStruct((tok_rows, width),...]
    unnamed x14 -> x12, local copies, waits for them, and re-layouts: 9.48 us -> 7.89 us
where the time goes in v2:
time: 138 us; the launch traced here: 137 us
  Pallas kernels  129 us (93%)
  local copies, waits for them, and re-layouts  7.89 us (6%)
    pallas_call x1, Pallas kernels, body(): pl.pallas_call(kernel, out_shape=(jax.ShapeDtypeStruct((tok_rows, width),...  129 us
    unnamed x12, local copies, waits for them, and re-layouts  7.89 us

profile of v2, /device:TPU:1, one launch (start us, length us, event | category | flops | bytes accessed | tf_op | source)
XLA Modules:
  0.0 137.1 jit_solution(3812747418376516814)
XLA Ops:
  0.6 0.0 copy-start
  0.6 0.9 copy-done
  1.6 0.0 copy-start.1
  1.6 0.9 copy-done.1
  2.5 0.0 copy-start.2
  2.5 0.7 copy-done.2
  3.2 0.0 copy-start.3
  3.2 0.7 copy-done.3
  3.9 128.5 %shard_map.102 = (bf16[128,1024]{1,0:T(8,128)(2,1)S(1)}, bf16[4096,256]{1,0:T(8,128)(2,1)S(1)}, bf16[4096,256]{1,0:T(8,128)(2,1)S(1)}, bf16[256,4096]{1,0:T(8,128)(2,1)S(1)}) custom-call(s32[2,128]{1,0:T(2,128)S(1)} %bitcast.11, bf16[2,128]{1,0:T(2,128)(2,1)S(1)} %bitcast.12, bf16[128,1024]{1,0:T(8,128)(2,1)S(1)} %copy-done, ...), custom_call_target="tpu_custom_call" | custom-call | tf_op jit(solution)/shard_map/pallas_call | solution.py:531
  132.4 0.7 copy.15
  133.1 1.3 copy.16
  134.4 1.3 copy.17
  135.8 1.3 copy.18
Async XLA Ops:
  0.6 1.0 copy-start
  1.6 0.9 copy-start.1
  2.5 0.7 copy-start.2
  3.2 0.7 copy-start.3

commit v3 on v2

--- a/solution.py
+++ b/solution.py
@@ -10,18 +10,27 @@
 ZS, XS, CORES = 8, 4, 2
 MESH = pl.DeviceIdType.MESH
 
-PLANE_OF = (2, 6, 5, 3, 7, 0, 4, 1)
-PLANE_CODE = sum(place << (3 * p) for p, place in enumerate(PLANE_OF))
-FAR, NEAR, SAME = 5, 3, 5
-SLOTS = 4
-
-SPREAD = (0, 1, 6)
-ONWARD = (3, 4, 9)
-UNPACK = (8, 9, 12)
-COMPUTE = (1, 2, 5, 6, 8, 9, 11, 12)
-REDUCE = (4, 5, 8, 10, 11, 12, 13, 15)
-GO_HOME = (7, 8, 10, 12, 13, 14, 15, 16)
-TURNS = 17
+PLANE_OF = (5, 3, 2, 6, 0, 4, 7, 1)
+FAR, NEAR, SAME = 5, 3, 4
+SLOTS = 6
+
+
+def code(items):
+    return sum(item << (3 * place) for place, item in enumerate(items))
+
+
+PLANE_CODE = code(PLANE_OF)
+
+GATHER_DONE = ((2,), (4,))
+SEND_NEAR = ((2, 4, 6), (0, 1, 2))
+ONWARD = ((2, 3, 6, 7, 8), (3, 1, 0, 2, 4))
+SPREAD = ((0, 1, 4, 5, 7), (3, 1, 0, 2, 4))
+UNPACK = ((7, 11, 12), (0, 2, 1))
+COMPUTE = ((7, 8, 10, 15), (0, 1, 2, 3))
+REDUCE = ((8, 9, 10, 12, 13, 14, 17, 18), (1, 0, 2, 5, 4, 3, 6, 7))
+GO_HOME = ((10, 11, 14, 15, 16, 19, 20, 21), (1, 0, 2, 5, 3, 6, 4, 7))
+WEIGHTS = ((17, 18), (0, 1))
+TURNS = 22
 
 
 def dot_last(left, right):
@@ -37,13 +46,13 @@
 
 
 def kernel(
-    ids_ref, weights_ref, tokens_ref, grad_ref, gate_hbm, up_hbm, down_hbm,
+    table_ref, both_ref, gate_hbm, up_hbm, down_hbm,
     out_tokens, out_gate, out_up, out_down,
-    dense, far_send, far_recv, near_send, near_recv, tok, sca, wgu, wdn, hid, act, part,
+    dense, far_send, far_recv, near_send, near_recv, tok, sca, wgu, wdn, hid, act, act_turned, part,
     pair_send, pair_recv, sum_send, sum_recv, home_send, home,
     weight_sems, dense_out, dense_sems, far_out, far_sems, near_out, near_sems,
     own_out, onward_out, row_sems, pair_out, pair_sems, sum_out, sum_sems,
-    home_out, home_sem, write_sems,
+    home_out, home_sems, write_sems,
 ):
     rank = lax.axis_index("expert")
     y = lax.axis_index("dp")
@@ -53,7 +62,7 @@
     zi, xi, ci = rank // plane, (rank // CORES) % XS, rank % CORES
     right, left = (y + 1) % PARTS, (y + PARTS - 1) % PARTS
     across = (y + 2) % PARTS
-    tok_rows, width = tokens_ref.shape
+    tok_rows, width = both_ref.shape[0] // 2, both_ref.shape[1]
     half = width // 2
     hidden = act.shape[1]
 
@@ -64,10 +73,10 @@
         return (PLANE_CODE >> (3 * p)) % 8
 
     def far_block(j):
-        return j + 2 * (j // 4)
+        return j + j // 4
 
     def near_block(n):
-        return 4 + n + n // 2
+        return 4 + n + (n + 1) // 2
 
     def peer(p, i, sign):
         z = (zi + sign * offset(p) + ZS) % ZS
@@ -101,8 +110,7 @@
     for copy in weight_copies:
         copy.start()
 
-    dense[y, pl.ds(0, tok_rows), :] = tokens_ref[...]
-    dense[y, pl.ds(tok_rows, tok_rows), :] = grad_ref[...]
+    dense[y] = both_ref[...]
 
     def dense_copy(h, q, out, arrive, side):
         block = dense.at[q, pl.ds(h * tok_rows, tok_rows)]
@@ -125,8 +133,8 @@
     def dense_arrival(h, q, arrive):
         dense_copy(h, q, dense_out.at[0], arrive, right).wait_recv()
 
-    ids, weights = ids_ref[...], weights_ref[...].astype(jnp.float32)
-    numbers = lax.broadcasted_iota(jnp.int32, (experts, tok_rows), 0)
+    ids, weights = table_ref[0:2], table_ref[2:4]
+    numbers = lax.broadcasted_iota(jnp.int32, (experts, tok_rows), 0).astype(jnp.float32)
     hits = [numbers == ids[c : c + 1] for c in range(2)]
     before = lax.broadcasted_iota(jnp.int32, (tok_rows, tok_rows), 0) < (
         lax.broadcasted_iota(jnp.int32, (tok_rows, tok_rows), 1)
@@ -138,7 +146,7 @@
     )
     place = [
         jnp.sum(jnp.where(hits[c], earlier, 0.0), axis=0, keepdims=True)
-        + ids[c : c + 1].astype(jnp.float32) * (2 * CAP)
+        + ids[c : c + 1] * (2 * CAP)
         for c in range(2)
     ]
 
@@ -195,7 +203,7 @@
             near_out.at[n], near_sems.at[n], (right, rank),
         )
 
-    def dispatch_near(n, carry):
+    def dispatch_near(n):
         which = picks(near_block(n))
         for q in range(PARTS):
             near_send[n, :, q] = pick(which, q)
@@ -214,8 +222,6 @@
         @pl.when(jnp.logical_not(same))
         def _():
             lax.fori_loop(0, plane, one, 0)
-
-        return carry
 
     def side_copy(buf, q, p, out, arrive, side):
         block = buf.at[q, at(p, rows)]
@@ -287,19 +293,26 @@
             (side, rank),
         )
 
-    def compute(p):
-        mine = at(p, rows)
-
-        @pl.when((p < 4) | (p == 6))
-        def _():
-            j = p - 2 * (p // 6)
+    def compute(pair):
+        mine = at(pair, 2 * rows)
+
+        def gathered(j):
             arrival(sca, left, j, 1)
             arrival(tok, right, j, 2)
             arrival(tok, across, j, 4)
             arrival(sca, across, j, 5)
 
-        pre = jnp.zeros((rows, 2 * hidden), jnp.float32)
-        grad_act = jnp.zeros((rows, hidden), jnp.float32)
+        @pl.when(pair < 2)
+        def _():
+            gathered(2 * pair)
+            gathered(2 * pair + 1)
+
+        @pl.when(pair == 2)
+        def _():
+            gathered(4)
+
+        pre = jnp.zeros((2 * rows, 2 * hidden), jnp.float32)
+        grad_act = jnp.zeros((2 * rows, hidden), jnp.float32)
         for q in range(PARTS):
             pre += jnp.dot(
                 tok[q, mine, :], wgu[pl.ds(q * width, width), :],
@@ -322,14 +335,16 @@
             return dot_last(hid[mine, :], wgu[at(q, width), :])
 
         far = back(across).astype(jnp.bfloat16)
-        pair_send[0, p] = far[:, :half]
-        pair_send[1, p] = far[:, half:]
-        pair_copy(0, p, right).start()
-        pair_copy(1, p, left).start()
-        slot = p % SLOTS
-        part[slot, 0] = back(right)
-        part[slot, 1] = back(left)
-        part[slot, 2] = back(y)
+        for i in range(2):
+            p = 2 * pair + i
+            pair_send[0, p] = far[i * rows : (i + 1) * rows, :half]
+            pair_send[1, p] = far[i * rows : (i + 1) * rows, half:]
+            pair_copy(0, p, right).start()
+            pair_copy(1, p, left).start()
+        for kept, q in enumerate((right, left, y)):
+            mine_part = back(q)
+            for i in range(2):
+                part[(2 * pair + i) % SLOTS, kept] = mine_part[i * rows : (i + 1) * rows]
 
     def reduce_sides(p):
         slot = p % SLOTS
@@ -348,7 +363,7 @@
 
     def home_copy(p, i):
         return remote(
-            home_send.at[p * plane + i], home.at[rank], home_out.at[p], home_sem.at[0],
+            home_send.at[p * plane + i], home.at[rank], home_out.at[p], home_sems.at[p],
             (y, peer(p, i, 1)),
         )
 
@@ -378,7 +393,7 @@
             lax.fori_loop(0, plane, one, 0)
 
     def write_copies(q):
-        lines = pl.ds(q * width, width)
+        lines = at(q, width)
         return [
             pltpu.make_async_copy(
                 wgu.at[lines, pl.ds(0, hidden)], out_gate.at[lines], write_sems.at[0, q]
@@ -392,89 +407,87 @@
     def weight_grads(q):
         tile = min(256, width)
 
+        def turned(block):
+            size = block.shape[1]
+            diagonal = lax.broadcasted_iota(jnp.int32, (size, size), 0) == (
+                lax.broadcasted_iota(jnp.int32, (size, size), 1)
+            )
+            unit = jnp.where(diagonal, 1.0, 0.0).astype(jnp.bfloat16)
+            return dot_last(unit, block).astype(jnp.bfloat16)
+
+        @pl.when(q == 0)
+        def _():
+            act_turned[...] = turned(act[...])
+
         def one(j, carry):
             cols = at(j, tile)
             lines = pl.ds(pl.multiple_of(q * width + j * tile, tile), tile)
-            wgu[lines, :] = dot_rows(tok[q, :, cols], hid[...]).astype(jnp.bfloat16)
-            wdn[:, lines] = dot_rows(act[...], sca[q, :, cols]).astype(jnp.bfloat16)
+            wgu[lines, :] = jnp.dot(
+                turned(tok[q, :, cols]), hid[...], preferred_element_type=jnp.float32
+            ).astype(jnp.bfloat16)
+            wdn[:, lines] = jnp.dot(
+                act_turned[...], sca[q, :, cols], preferred_element_type=jnp.float32
+            ).astype(jnp.bfloat16)
             return carry
 
         lax.fori_loop(0, width // tile, one, 0)
         for copy in write_copies(q):
             copy.start()
 
-    pack_far(0)
+    def next_far(j, carry):
+        pack_far(j)
+        return dispatch_far(j, carry)
+
+    pack_far(1)
     pl.semaphore_wait(barrier, experts + 1)
     for copy in dense_own():
         copy.start()
-    dispatch_far(0, 0)
-
-    def next_far(j, carry):
-        pack_far(j)
-        return dispatch_far(j, carry)
-
-    lax.fori_loop(1, 3, next_far, 0)
+    dispatch_far(1, 0)
+    lax.fori_loop(2, 4, next_far, 0)
     copies = dense_onward()
     dense_arrival(0, left, 0)
     copies[0].start()
     dense_arrival(1, right, 3)
     copies[1].start()
-    lax.fori_loop(3, FAR, next_far, 0)
+    next_far(0, 0)
     for copy in weight_copies:
         copy.wait()
 
-    def next_spread(j, carry):
-        spread(j)
-        return carry
-
-    def next_onward(j, carry):
-        onward(j)
-        return carry
-
-    lax.fori_loop(0, 2, next_spread, 0)
-    dense_arrival(1, left, 1)
-    dense_arrival(0, right, 2)
-    dense_arrival(0, across, 4)
-    dense_arrival(1, across, 5)
-    lax.fori_loop(0, NEAR, dispatch_near, 0)
-    lax.fori_loop(0, 2, next_onward, 0)
+    def gather_done(j):
+        dense_arrival(1, left, 1)
+        dense_arrival(0, right, 2)
+        dense_arrival(0, across, 4)
+        dense_arrival(1, across, 5)
+        next_far(j, 0)
 
     def turn(t, carry):
-        def stage(turns, work, done):
+        def stage(plan, work):
+            turns, blocks = plan
             now = t == turns[0]
             for at_turn in turns[1:]:
                 now = now | (t == at_turn)
 
             @pl.when(now)
             def _():
-                index = done
+                index = 0
                 for at_turn in turns:
                     index = index + jnp.where(t > at_turn, 1, 0)
-                work(index)
-
-        stage(ONWARD, onward, 2)
-        stage(REDUCE, reduce_sides, 0)
-        stage(GO_HOME, go_home, 0)
-        stage(SPREAD, spread, 2)
-        stage(UNPACK, unpack, 0)
-        stage(COMPUTE, compute, 0)
+                work((code(blocks) >> (3 * index)) % 8)
+
+        stage(GATHER_DONE, gather_done)
+        stage(SEND_NEAR, dispatch_near)
+        stage(ONWARD, onward)
+        stage(SPREAD, spread)
+        stage(UNPACK, unpack)
+        stage(COMPUTE, compute)
+        stage(REDUCE, reduce_sides)
+        stage(GO_HOME, go_home)
+        stage(WEIGHTS, weight_grads)
         return carry
 
     lax.fori_loop(0, TURNS, turn, 0)
-    for q in range(PARTS):
+    for q in range(len(WEIGHTS[0]), PARTS):
         weight_grads(q)
-
-    remote(
-        home_send.at[pl.ds(0, experts - 1)], home.at[pl.ds(0, experts - 1)],
-        home_out.at[0], home_sem.at[0], (right, rank),
-    ).wait_recv()
-    result = jnp.zeros((2 * tok_rows, half), jnp.float32)
-    for z in range(ZS):
-        block = home[pl.ds(z * plane, plane)].reshape(plane * 2 * CAP, half)
-        result += dot_rows(chosen(z, ones, ones), block)
-    result = result.astype(jnp.bfloat16)
-    out_tokens[:, pl.ds(0, half)] = result[:tok_rows]
-    out_tokens[:, pl.ds(half, half)] = result[tok_rows:]
 
     for copy in dense_own() + dense_onward():
         copy.wait_send()
@@ -489,17 +502,32 @@
     for n in range(NEAR):
         near_whole(n, 1 if near_block(n) == SAME else 0).wait_send()
 
+    def finish_sides(p, carry):
+        for s, side in ((0, right), (1, left)):
+            pair_copy(s, p, side).wait_send()
+            sum_copy(s, p, side).wait_send()
+        return carry
+
+    lax.fori_loop(0, ZS, finish_sides, 0)
+
+    result = jnp.zeros((2 * tok_rows, half), jnp.float32)
+    for p in GO_HOME[1]:
+        z = (zi - offset(p) + ZS) % ZS
+        some = home.at[pl.ds(0, plane - 1 if p == SAME else plane)]
+        remote(some, some, home_out.at[p], home_sems.at[p], (right, rank)).wait_recv()
+        block = home[at(z, plane)].reshape(plane * 2 * CAP, half)
+        result += dot_rows(chosen(z, ones, ones), block)
+    result = result.astype(jnp.bfloat16)
+    out_tokens[:, pl.ds(0, half)] = result[:tok_rows]
+    out_tokens[:, pl.ds(half, half)] = result[tok_rows:]
+
     def home_sent(p, count):
         some = pl.ds(0, count)
         remote(
-            home_send.at[some], home.at[some], home_out.at[p], home_sem.at[0], (right, rank)
+            home_send.at[some], home.at[some], home_out.at[p], home_sems.at[p], (right, rank)
         ).wait_send()
 
     def finish(p, carry):
-        for s, side in ((0, right), (1, left)):
-            pair_copy(s, p, side).wait_send()
-            sum_copy(s, p, side).wait_send()
-
         @pl.when(p == SAME)
         def _():
             home_sent(p, plane - 1)
@@ -514,6 +542,23 @@
     for q in range(PARTS):
         for copy in write_copies(q):
             copy.wait()
+
+
+def write_out(*refs):
+    count = (len(refs) - 1) // 2
+    sources, targets, sems = refs[:count], refs[count : 2 * count], refs[-1]
+    copies = []
+    for number, (source, target) in enumerate(zip(sources, targets)):
+        step = source.shape[0] // PARTS
+        for piece in range(PARTS):
+            lines = pl.ds(piece * step, step)
+            copies.append(
+                pltpu.make_async_copy(source.at[lines], target.at[lines], sems.at[number, piece])
+            )
+    for copy in copies:
+        copy.start()
+    for copy in copies:
+        copy.wait()
 
 
 def body(tokens, grad_out, route_weights, expert_ids, gate_weight, up_weight, down_weight):
@@ -536,7 +581,7 @@
             jax.ShapeDtypeStruct((features, hidden), bf16),
             jax.ShapeDtypeStruct((hidden, features), bf16),
         ),
-        in_specs=[vmem, vmem, vmem, vmem, hbm, hbm, hbm],
+        in_specs=[vmem, vmem, hbm, hbm, hbm],
         out_specs=(vmem, free, free, free),
         scratch_shapes=[
             pltpu.VMEM((PARTS, 2 * tok_rows, width), bf16),
@@ -550,6 +595,7 @@
             pltpu.VMEM((hidden, features), bf16),
             pltpu.VMEM((total, 2 * hidden), bf16),
             pltpu.VMEM((total, hidden), bf16),
+            pltpu.VMEM((hidden, total), bf16),
             pltpu.VMEM((SLOTS, 3, rows, width), f32),
             pltpu.VMEM((2, ZS, rows, half), bf16),
             pltpu.VMEM((2, ZS, rows, half), bf16),
@@ -572,16 +618,25 @@
             dma((2, ZS)),
             dma((2, ZS)),
             dma((ZS,)),
-            dma((1,)),
+            dma((ZS,)),
             dma((3, PARTS)),
         ],
         compiler_params=pltpu.CompilerParams(
             collective_id=0, has_side_effects=True, vmem_limit_bytes=47 * 1024 * 1024
         ),
     )(
-        expert_ids.T, route_weights.T, tokens, grad_out,
+        jnp.concatenate([expert_ids.T.astype(f32), route_weights.T.astype(f32)], axis=0),
+        jnp.concatenate([tokens, grad_out], axis=0),
         gate_weight[0], up_weight[0], down_weight[0],
     )
+    grads = pl.pallas_call(
+        write_out,
+        out_shape=tuple(jax.ShapeDtypeStruct(array.shape, bf16) for array in grads),
+        in_specs=[free] * 4,
+        out_specs=(free,) * 4,
+        scratch_shapes=[dma((4, PARTS))],
+        compiler_params=pltpu.CompilerParams(vmem_limit_bytes=2 * 1024 * 1024),
+    )(*grads)
     return (grads[0], grads[1][None], grads[2][None], grads[3][None])
 
 

time: 138 us -> 129 us (0.935)
  local copies, waits for them, and re-layouts: 7.89 us -> 0 us
  Pallas kernels: 129 us -> 126 us
  other arithmetic: 0 us -> 2.41 us
    unnamed x12 -> x0, local copies, waits for them, and re-layouts: 7.89 us -> none
    pallas_call x1, Pallas kernels: 129 us -> 123 us  [body(): pl.pallas_call(kernel, out_shape=(jax.ShapeDtypeStruct((tok_rows, width),...]
    pallas_call x0 -> x1, Pallas kernels: none -> 2.87 us  [body(): pl.pallas_call(write_out, out_shape=tuple((jax.ShapeDtypeStruct(array.sha...]
where the time goes in v3:
time: 129 us
  Pallas kernels  126 us (98%)
  other arithmetic  2.41 us (2%)
    pallas_call x1, Pallas kernels, body(): pl.pallas_call(kernel, out_shape=(jax.ShapeDtypeStruct((tok_rows, width),...  123 us
    pallas_call x1, Pallas kernels, body(): pl.pallas_call(write_out, out_shape=tuple((jax.ShapeDtypeStruct(array.sha...  2.87 us

profile of v3, /device:TPU:1, one launch (start us, length us, event | category | flops | bytes accessed | tf_op | source)
XLA Modules:
  0.0 128.9 jit_solution(12445301375178934244)
XLA Ops:
  0.6 0.7 convert_bitcast_fusion
  1.3 0.7 convert_bitcast_fusion.1
  2.0 1.1 pad_maximum_fusion.both_ref
  3.0 122.9 %shard_map.102 = (bf16[128,1024]{1,0:T(8,128)(2,1)S(1)}, bf16[4096,256]{1,0:T(8,128)(2,1)S(1)}, bf16[4096,256]{1,0:T(8,128)(2,1)S(1)}, bf16[256,4096]{1,0:T(8,128)(2,1)S(1)}) custom-call(f32[4,128]{1,0:T(4,128)S(1)} %pad_maximum_fusion.1.table_ref, bf16[256,1024]{1,0:T(8,128)(2,1)S(1)} %pad_maximum_fusion.both_ref, bf16[4096,256]{1,0:T(8,128)(2,1)} %bitcast.10, ...), custom_call_target="tpu_custom_call" | custom-call | tf_op jit(solution)/shard_map/pallas_call | solution.py:576
  126.0 2.9 %shard_map.103 = (bf16[128,1024]{1,0:T(8,128)(2,1)}, bf16[4096,256]{1,0:T(8,128)(2,1)}, bf16[4096,256]{1,0:T(8,128)(2,1)}, bf16[256,4096]{1,0:T(8,128)(2,1)}) custom-call(bf16[128,1024]{1,0:T(8,128)(2,1)S(1)} %get-tuple-element.12.refs_0_, bf16[4096,256]{1,0:T(8,128)(2,1)S(1)} %get-tuple-element.13.refs_1_, bf16[4096,256]{1,0:T(8,128)(2,1)S(1)} %get-tuple-element.14.refs_2_, ...), custom_call_target="tpu_custom_call" | custom-call | tf_op jit(solution)/shard_map/pallas_call | solution.py:632
  (1 shorter events, 0.0 us)

commit v4 on v3

--- a/solution.py
+++ b/solution.py
@@ -29,6 +29,7 @@
 COMPUTE = ((7, 8, 10, 15), (0, 1, 2, 3))
 REDUCE = ((8, 9, 10, 12, 13, 14, 17, 18), (1, 0, 2, 5, 4, 3, 6, 7))
 GO_HOME = ((10, 11, 14, 15, 16, 19, 20, 21), (1, 0, 2, 5, 3, 6, 4, 7))
+TURN_WEIGHTS = ((0, 1, 3, 5), (0, 1, 2, 3))
 WEIGHTS = ((17, 18), (0, 1))
 TURNS = 22
 
@@ -39,6 +40,15 @@
     )
 
 
+def turned(block):
+    size = block.shape[1]
+    diagonal = lax.broadcasted_iota(jnp.int32, (size, size), 0) == (
+        lax.broadcasted_iota(jnp.int32, (size, size), 1)
+    )
+    unit = jnp.where(diagonal, 1.0, 0.0).astype(jnp.bfloat16)
+    return dot_last(unit, block).astype(jnp.bfloat16)
+
+
 def dot_rows(left, right):
     return lax.dot_general(
         left, right, (((0,), (0,)), ((), ())), preferred_element_type=jnp.float32
@@ -48,7 +58,7 @@
 def kernel(
     table_ref, both_ref, gate_hbm, up_hbm, down_hbm,
     out_tokens, out_gate, out_up, out_down,
-    dense, far_send, far_recv, near_send, near_recv, tok, sca, wgu, wdn, hid, act, act_turned, part,
+    dense, far_send, far_recv, near_send, near_recv, tok, sca, wgu, wdn, wgu_turned, wdn_turned, hid, act, act_turned, part,
     pair_send, pair_recv, sum_send, sum_recv, home_send, home,
     weight_sems, dense_out, dense_sems, far_out, far_sems, near_out, near_sems,
     own_out, onward_out, row_sems, pair_out, pair_sems, sum_out, sum_sems,
@@ -110,11 +120,12 @@
     for copy in weight_copies:
         copy.start()
 
-    dense[y] = both_ref[...]
-
     def dense_copy(h, q, out, arrive, side):
-        block = dense.at[q, pl.ds(h * tok_rows, tok_rows)]
-        return remote(block, block, out, dense_sems.at[arrive], (side, rank))
+        some = pl.ds(h * tok_rows, tok_rows)
+        return remote(
+            both_ref.at[some] if q is y else dense.at[q, some], dense.at[q, some],
+            out, dense_sems.at[arrive], (side, rank),
+        )
 
     def dense_own():
         return [
@@ -133,7 +144,13 @@
     def dense_arrival(h, q, arrive):
         dense_copy(h, q, dense_out.at[0], arrive, right).wait_recv()
 
-    ids, weights = table_ref[0:2], table_ref[2:4]
+    pl.semaphore_wait(barrier, experts + 1)
+    for copy in dense_own():
+        copy.start()
+    dense[y] = both_ref[...]
+
+    ids = jnp.floor(table_ref[...] * 0.5)
+    weights = table_ref[...] - 2.0 * ids
     numbers = lax.broadcasted_iota(jnp.int32, (experts, tok_rows), 0).astype(jnp.float32)
     hits = [numbers == ids[c : c + 1] for c in range(2)]
     before = lax.broadcasted_iota(jnp.int32, (tok_rows, tok_rows), 0) < (
@@ -293,6 +310,19 @@
             (side, rank),
         )
 
+    def turn_weights(q):
+        tile = min(256, width)
+
+        def one(j, carry):
+            lines = pl.ds(pl.multiple_of(q * width + j * tile, tile), tile)
+            for h in range(2):
+                some = pl.ds(h * hidden, hidden)
+                wgu_turned[some, lines] = turned(wgu[lines, some])
+            wdn_turned[lines, :] = turned(wdn[:, lines])
+            return carry
+
+        lax.fori_loop(0, width // tile, one, 0)
+
     def compute(pair):
         mine = at(pair, 2 * rows)
 
@@ -318,7 +348,10 @@
                 tok[q, mine, :], wgu[pl.ds(q * width, width), :],
                 preferred_element_type=jnp.float32,
             )
-            grad_act += dot_last(sca[q, mine, :], wdn[:, pl.ds(q * width, width)])
+            grad_act += jnp.dot(
+                sca[q, mine, :], wdn_turned[pl.ds(q * width, width), :],
+                preferred_element_type=jnp.float32,
+            )
         gate_pre, up_pre = pre[:, :hidden], pre[:, hidden:]
         sigmoid_gate = 1.0 / (1.0 + jnp.exp(-gate_pre))
         swish_gate = gate_pre * sigmoid_gate
@@ -332,7 +365,9 @@
         ).astype(jnp.bfloat16)
 
         def back(q):
-            return dot_last(hid[mine, :], wgu[at(q, width), :])
+            return jnp.dot(
+                hid[mine, :], wgu_turned[:, at(q, width)], preferred_element_type=jnp.float32
+            )
 
         far = back(across).astype(jnp.bfloat16)
         for i in range(2):
@@ -407,14 +442,6 @@
     def weight_grads(q):
         tile = min(256, width)
 
-        def turned(block):
-            size = block.shape[1]
-            diagonal = lax.broadcasted_iota(jnp.int32, (size, size), 0) == (
-                lax.broadcasted_iota(jnp.int32, (size, size), 1)
-            )
-            unit = jnp.where(diagonal, 1.0, 0.0).astype(jnp.bfloat16)
-            return dot_last(unit, block).astype(jnp.bfloat16)
-
         @pl.when(q == 0)
         def _():
             act_turned[...] = turned(act[...])
@@ -438,12 +465,7 @@
         pack_far(j)
         return dispatch_far(j, carry)
 
-    pack_far(1)
-    pl.semaphore_wait(barrier, experts + 1)
-    for copy in dense_own():
-        copy.start()
-    dispatch_far(1, 0)
-    lax.fori_loop(2, 4, next_far, 0)
+    lax.fori_loop(1, 4, next_far, 0)
     copies = dense_onward()
     dense_arrival(0, left, 0)
     copies[0].start()
@@ -482,6 +504,7 @@
         stage(COMPUTE, compute)
         stage(REDUCE, reduce_sides)
         stage(GO_HOME, go_home)
+        stage(TURN_WEIGHTS, turn_weights)
         stage(WEIGHTS, weight_grads)
         return carry
 
@@ -593,6 +616,8 @@
             pltpu.VMEM((PARTS, total, width), bf16),
             pltpu.VMEM((features, 2 * hidden), bf16),
             pltpu.VMEM((hidden, features), bf16),
+            pltpu.VMEM((2 * hidden, features), bf16),
+            pltpu.VMEM((features, hidden), bf16),
             pltpu.VMEM((total, 2 * hidden), bf16),
             pltpu.VMEM((total, hidden), bf16),
             pltpu.VMEM((hidden, total), bf16),
@@ -625,7 +650,7 @@
             collective_id=0, has_side_effects=True, vmem_limit_bytes=47 * 1024 * 1024
         ),
     )(
-        jnp.concatenate([expert_ids.T.astype(f32), route_weights.T.astype(f32)], axis=0),
+        (2.0 * expert_ids.astype(f32) + route_weights.astype(f32)).T,
         jnp.concatenate([tokens, grad_out], axis=0),
         gate_weight[0], up_weight[0], down_weight[0],
     )

time: 129 us -> 129 us (level)
    convert_element_type x2 -> x0, other arithmetic: 1.34 us -> none  [the longest x1 0.68 us: body(): expert_ids.T.astype(f32)]
where the time goes in v4:
time: 129 us
  Pallas kernels  126 us (98%)
  other arithmetic  1.76 us (1%)
    pallas_call x1, Pallas kernels, body(): pl.pallas_call(kernel, out_shape=(jax.ShapeDtypeStruct((tok_rows, width),...  124 us
    pallas_call x1, Pallas kernels, body(): pl.pallas_call(write_out, out_shape=tuple((jax.ShapeDtypeStruct(array.sha...  2.87 us

profile of v4, /device:TPU:1, one launch (start us, length us, event | category | flops | bytes accessed | tf_op | source)
XLA Modules:
  0.0 128.9 jit_solution(1427891823006883685)
XLA Ops:
  0.6 0.7 add_bitcast_fusion.table_ref
  1.3 1.1 pad_maximum_fusion.both_ref
  2.4 123.6 %shard_map.102 = (bf16[128,1024]{1,0:T(8,128)(2,1)S(1)}, bf16[4096,256]{1,0:T(8,128)(2,1)S(1)}, bf16[4096,256]{1,0:T(8,128)(2,1)S(1)}, bf16[256,4096]{1,0:T(8,128)(2,1)S(1)}) custom-call(f32[2,128]{1,0:T(2,128)S(1)} %add_bitcast_fusion.table_ref, bf16[256,1024]{1,0:T(8,128)(2,1)S(1)} %pad_maximum_fusion.both_ref, bf16[4096,256]{1,0:T(8,128)(2,1)} %bitcast.8, ...), custom_call_target="tpu_custom_call" | custom-call | tf_op jit(solution)/shard_map/pallas_call | solution.py:599
  126.0 2.9 %shard_map.103 = (bf16[128,1024]{1,0:T(8,128)(2,1)}, bf16[4096,256]{1,0:T(8,128)(2,1)}, bf16[4096,256]{1,0:T(8,128)(2,1)}, bf16[256,4096]{1,0:T(8,128)(2,1)}) custom-call(bf16[128,1024]{1,0:T(8,128)(2,1)S(1)} %get-tuple-element.12.refs_0_, bf16[4096,256]{1,0:T(8,128)(2,1)S(1)} %get-tuple-element.13.refs_1_, bf16[4096,256]{1,0:T(8,128)(2,1)S(1)} %get-tuple-element.14.refs_2_, ...), custom_call_target="tpu_custom_call" | custom-call | tf_op jit(solution)/shard_map/pallas_call | solution.py:657

commit v5 on v4

--- a/solution.py
+++ b/solution.py
@@ -22,16 +22,16 @@
 PLANE_CODE = code(PLANE_OF)
 
 GATHER_DONE = ((2,), (4,))
-SEND_NEAR = ((2, 4, 6), (0, 1, 2))
+SEND_NEAR = ((2, 3, 4, 5, 6, 7), (0, 1, 2, 3, 4, 5))
 ONWARD = ((2, 3, 6, 7, 8), (3, 1, 0, 2, 4))
 SPREAD = ((0, 1, 4, 5, 7), (3, 1, 0, 2, 4))
-UNPACK = ((7, 11, 12), (0, 2, 1))
-COMPUTE = ((7, 8, 10, 15), (0, 1, 2, 3))
-REDUCE = ((8, 9, 10, 12, 13, 14, 17, 18), (1, 0, 2, 5, 4, 3, 6, 7))
-GO_HOME = ((10, 11, 14, 15, 16, 19, 20, 21), (1, 0, 2, 5, 3, 6, 4, 7))
+UNPACK = ((7, 15, 16), (0, 2, 1))
+COMPUTE = ((7, 8, 10, 16), (0, 1, 2, 3))
+REDUCE = ((8, 9, 10, 12, 13, 14, 18, 19), (1, 0, 2, 5, 4, 3, 6, 7))
+GO_HOME = ((10, 11, 14, 16, 17, 20, 21, 22), (1, 0, 2, 5, 3, 6, 4, 7))
 TURN_WEIGHTS = ((0, 1, 3, 5), (0, 1, 2, 3))
-WEIGHTS = ((17, 18), (0, 1))
-TURNS = 22
+WEIGHTS = ((18, 19), (0, 1))
+TURNS = 23
 
 
 def dot_last(left, right):
@@ -108,9 +108,9 @@
         )
         return carry
 
-    lax.fori_loop(1, experts, greet, 0)
     for side in (left, right):
         pl.semaphore_signal(barrier, inc=1, device_id=(side, rank), device_id_type=MESH)
+    lax.fori_loop(1, experts, greet, 0)
 
     weight_copies = [
         pltpu.make_async_copy(gate_hbm, wgu.at[:, pl.ds(0, hidden)], weight_sems.at[0]),
@@ -220,25 +220,25 @@
             near_out.at[n], near_sems.at[n], (right, rank),
         )
 
-    def dispatch_near(n):
-        which = picks(near_block(n))
-        for q in range(PARTS):
-            near_send[n, :, q] = pick(which, q)
+    def dispatch_near(m):
+        n, second = m // 2, m % 2
+
+        @pl.when(second == 0)
+        def _():
+            which = picks(near_block(n))
+            for q in range(PARTS):
+                near_send[n, :, q] = pick(which, q)
 
         def one(i, inner):
             near_copy(n, i).start()
             return inner
 
-        same = near_block(n) == SAME
-
-        @pl.when(same)
-        def _():
-            near_recv[n, 0] = near_send[n, rank % plane]
-            lax.fori_loop(1, plane, one, 0)
-
-        @pl.when(jnp.logical_not(same))
-        def _():
-            lax.fori_loop(0, plane, one, 0)
+        @pl.when(m == 0)
+        def _():
+            near_recv[0, 0] = near_send[0, rank % plane]
+
+        first = second * (plane // 2)
+        lax.fori_loop(jnp.where(m == 0, 1, first), first + plane // 2, one, 0)
 
     def side_copy(buf, q, p, out, arrive, side):
         block = buf.at[q, at(p, rows)]

time: 129 us -> 122 us (0.946)
  Pallas kernels: 126 us -> 119 us
    pallas_call x1, Pallas kernels: 124 us -> 117 us  [body(): pl.pallas_call(kernel, out_shape=(jax.ShapeDtypeStruct((tok_rows, width),...]
where the time goes in v5:
time: 122 us
  Pallas kernels  119 us (98%)
  other arithmetic  1.76 us (1%)
    pallas_call x1, Pallas kernels, body(): pl.pallas_call(kernel, out_shape=(jax.ShapeDtypeStruct((tok_rows, width),...  117 us
    pallas_call x1, Pallas kernels, body(): pl.pallas_call(write_out, out_shape=tuple((jax.ShapeDtypeStruct(array.sha...  2.87 us

profile of v5, /device:TPU:1, one launch (start us, length us, event | category | flops | bytes accessed | tf_op | source)
XLA Modules:
  0.0 121.9 jit_solution(8724914761251717447)
XLA Ops:
  0.6 0.7 add_bitcast_fusion.table_ref
  1.3 1.1 pad_maximum_fusion.both_ref
  2.4 116.6 %shard_map.102 = (bf16[128,1024]{1,0:T(8,128)(2,1)S(1)}, bf16[4096,256]{1,0:T(8,128)(2,1)S(1)}, bf16[4096,256]{1,0:T(8,128)(2,1)S(1)}, bf16[256,4096]{1,0:T(8,128)(2,1)S(1)}) custom-call(f32[2,128]{1,0:T(2,128)S(1)} %add_bitcast_fusion.table_ref, bf16[256,1024]{1,0:T(8,128)(2,1)S(1)} %pad_maximum_fusion.both_ref, bf16[4096,256]{1,0:T(8,128)(2,1)} %bitcast.8, ...), custom_call_target="tpu_custom_call" | custom-call | tf_op jit(solution)/shard_map/pallas_call | solution.py:599
  119.0 2.9 %shard_map.103 = (bf16[128,1024]{1,0:T(8,128)(2,1)}, bf16[4096,256]{1,0:T(8,128)(2,1)}, bf16[4096,256]{1,0:T(8,128)(2,1)}, bf16[256,4096]{1,0:T(8,128)(2,1)}) custom-call(bf16[128,1024]{1,0:T(8,128)(2,1)S(1)} %get-tuple-element.12.refs_0_, bf16[4096,256]{1,0:T(8,128)(2,1)S(1)} %get-tuple-element.13.refs_1_, bf16[4096,256]{1,0:T(8,128)(2,1)S(1)} %get-tuple-element.14.refs_2_, ...), custom_call_target="tpu_custom_call" | custom-call | tf_op jit(solution)/shard_map/pallas_call | solution.py:657

commit v6 on v5

--- a/solution.py
+++ b/solution.py
@@ -22,10 +22,10 @@
 PLANE_CODE = code(PLANE_OF)
 
 GATHER_DONE = ((2,), (4,))
-SEND_NEAR = ((2, 3, 4, 5, 6, 7), (0, 1, 2, 3, 4, 5))
+SEND_NEAR = ((2, 3, 4, 5, 6, 7), (2, 4, 3, 5, 0, 1))
 ONWARD = ((2, 3, 6, 7, 8), (3, 1, 0, 2, 4))
 SPREAD = ((0, 1, 4, 5, 7), (3, 1, 0, 2, 4))
-UNPACK = ((7, 15, 16), (0, 2, 1))
+UNPACK = ((10, 15, 16), (0, 2, 1))
 COMPUTE = ((7, 8, 10, 16), (0, 1, 2, 3))
 REDUCE = ((8, 9, 10, 12, 13, 14, 18, 19), (1, 0, 2, 5, 4, 3, 6, 7))
 GO_HOME = ((10, 11, 14, 16, 17, 20, 21, 22), (1, 0, 2, 5, 3, 6, 4, 7))

time: 122 us -> 128 us (1.049)
  the two profiles are of different devices: /device:TPU:1 before, /device:TPU:134 now
where the time goes in v6:
time: 128 us
  Pallas kernels  126 us (98%)
  other arithmetic  1.76 us (1%)
    pallas_call x1, Pallas kernels, body(): pl.pallas_call(kernel, out_shape=(jax.ShapeDtypeStruct((tok_rows, width),...  123 us
    pallas_call x1, Pallas kernels, body(): pl.pallas_call(write_out, out_shape=tuple((jax.ShapeDtypeStruct(array.sha...  2.87 us

profile of v6, /device:TPU:134, one launch (start us, length us, event | category | flops | bytes accessed | tf_op | source)
XLA Modules:
  0.0 128.3 jit_solution(17211405487151528823)
XLA Ops:
  0.6 0.7 add_bitcast_fusion.table_ref
  1.3 1.1 pad_maximum_fusion.both_ref
  2.4 123.0 %shard_map.102 = (bf16[128,1024]{1,0:T(8,128)(2,1)S(1)}, bf16[4096,256]{1,0:T(8,128)(2,1)S(1)}, bf16[4096,256]{1,0:T(8,128)(2,1)S(1)}, bf16[256,4096]{1,0:T(8,128)(2,1)S(1)}) custom-call(f32[2,128]{1,0:T(2,128)S(1)} %add_bitcast_fusion.table_ref, bf16[256,1024]{1,0:T(8,128)(2,1)S(1)} %pad_maximum_fusion.both_ref, bf16[4096,256]{1,0:T(8,128)(2,1)} %bitcast.8, ...), custom_call_target="tpu_custom_call" | custom-call | tf_op jit(solution)/shard_map/pallas_call | solution.py:599
  125.4 2.9 %shard_map.103 = (bf16[128,1024]{1,0:T(8,128)(2,1)}, bf16[4096,256]{1,0:T(8,128)(2,1)}, bf16[4096,256]{1,0:T(8,128)(2,1)}, bf16[256,4096]{1,0:T(8,128)(2,1)}) custom-call(bf16[128,1024]{1,0:T(8,128)(2,1)S(1)} %get-tuple-element.12.refs_0_, bf16[4096,256]{1,0:T(8,128)(2,1)S(1)} %get-tuple-element.13.refs_1_, bf16[4096,256]{1,0:T(8,128)(2,1)S(1)} %get-tuple-element.14.refs_2_, ...), custom_call_target="tpu_custom_call" | custom-call | tf_op jit(solution)/shard_map/pallas_call | solution.py:657
